TPU v7x, 32 devices: a whole 2x2x4 slice. The times are simulated.
32 devices in a mesh: groups: 2 (over x), dp: 16 (over z, y, core).
Axes of the slice: x: 2, y: 2, z: 4, core: 2. Of those that a mesh axis runs over, the one named last changes fastest.
Arguments:
- queries: bfloat16 [16384, 1024], P(('groups', 'dp')), parts along dimension 0, may hold values from -5.5 to 5.5
- kv_cache: bfloat16 [16384, 256], P(('groups', 'dp')), parts along dimension 0, may hold values from -5.5 to 5.5
- grad_out: bfloat16 [16384, 1024], P(('groups', 'dp')), parts along dimension 0, may hold values from -48 to 48
- pair_lengths: int32 [20], P('groups'), parts along dimension 0, may hold values from 1 to 12, 32 in all
Outputs:
- grad_queries: bfloat16 [16384, 1024], P(('groups', 'dp')), parts along dimension 0
- grad_kv: float32 [16384, 256], P(('groups', 'dp')), parts along dimension 0
There are 2 independent parts, one for each index of `groups`. A program takes and returns all parts, laid end to end along the dimension named above; each array names one. Nothing has to cross between parts.
Inputs may be any that keep to these rules, and one draw needn't show every extreme that they name: `pair_lengths`: the 10 lengths sum to 32; the longest is exactly 12.
All inputs are finite; a program needn't handle non-finite values.
Results may differ from a plain program's by a relative error of at most 0.0078.
Values may be sent and summed in bfloat16 or wider, within the bound.
No kernel may reach another device: no remote copies, remote signals or barrier semaphores. Data moves between devices by JAX's collectives and lax.ppermute only.
A program may use at most 192 MiB of HBM per device.

v0:
```python
import functools

import jax
import jax.numpy as jnp
from jax import lax
from jax.experimental import pallas as pl
from jax.experimental.pallas import tpu as pltpu
from jax.sharding import PartitionSpec as P

HD = 128
QH = 8
HG = 4
TILE = 256
MOST = 12
FAR_STEPS = (8, 2, 1)
OWN_STEPS = (4, 2, 1)
REACH = 3
SCALE = HD**-0.5
SCALE_LOG2 = SCALE * 1.4426950408889634
F32 = jnp.float32
BF16 = jnp.bfloat16
GROUPS = QH // HG

ROUNDS = (("row", "two_rows"), ("up_across", "down_across"), ("up", "down"))


def chip_step(relation, column):
    return {
        "row": 1 - 2 * column,
        "up": 2,
        "down": -2,
        "up_across": 3 - 2 * column,
        "down_across": -1 - 2 * column,
        "two_rows": 6 * column - 3,
    }[relation]


class Place:
    def __init__(self, lengths, per_device, index):
        me = lax.axis_index("dp")
        per_chip = 2 * per_device
        tile = index // GROUPS
        self.group = index % GROUPS
        own_tile = me * per_device + tile
        first = jnp.int32(0)
        last = jnp.int32(0)
        end = jnp.int32(0)
        for pair in range(lengths.shape[0]):
            start = end
            end = start + lengths[pair]
            inside = (own_tile >= start) & (own_tile < end)
            first = jnp.where(inside, start, first)
            last = jnp.where(inside, end, last)
        chip_start = (me // 2) * per_chip
        chip_end = chip_start + per_chip
        below = jnp.maximum(chip_start - first, 0)
        above = jnp.maximum(last - chip_end, 0)
        self.far_base = REACH * per_chip - below
        self.far_count = below + above
        self.own_base = jnp.maximum(first, chip_start) - chip_start
        self.own_count = jnp.minimum(last, chip_end) - chip_start - self.own_base
        self.rows = pl.ds(pl.multiple_of(tile * TILE, TILE), TILE)
        self.slot = tile * QH + self.group * HG

    def cols(self, head):
        return pl.ds(pl.multiple_of((self.group * HG + head) * HD, HD), HD)


def tiles(block, blocks):
    return pl.ds(pl.multiple_of(block * TILE, TILE), blocks * TILE)


def sweep(count, sizes, step, state):
    done = 0
    for size in sizes:
        rounds = (count - done) // size
        state = lax.fori_loop(0, rounds, lambda i, s, d=done, n=size: step(d + i * n, n, s), state)
        done = done + rounds * size
    return state


def products(place, kv, at, q_t, g_t, head):
    score = jnp.dot(kv[at, :HD], q_t[head], preferred_element_type=F32)
    gprob = jnp.dot(kv[at, HD:], g_t[head], preferred_element_type=F32)
    return score, gprob


def gathered(state, score, gprob):
    top, total, weighted = state
    new_top = jnp.maximum(top, jnp.max(score, axis=0, keepdims=True))
    weight = jnp.exp2((score - new_top) * SCALE_LOG2)
    fade = jnp.exp2((top - new_top) * SCALE_LOG2)
    total = total * fade + jnp.sum(weight, axis=0, keepdims=True)
    weighted = weighted * fade + jnp.sum(weight * gprob, axis=0, keepdims=True)
    return (new_top, total, weighted), weight


def turn_rows(place, q_ref, g_ref, q_t, g_t):
    for head in range(HG):
        q_t[head] = q_ref[place.rows, place.cols(head)].T
        g_t[head] = g_ref[place.rows, place.cols(head)].T


def load_chip(chip_any, kv, sems, rows_dev, core):
    copies = []
    for half, which in enumerate((core, 1 - core)):
        to = pl.ds(pl.multiple_of(which * rows_dev, rows_dev), rows_dev)
        copies.append(
            pltpu.make_async_copy(chip_any.at[pl.ds(half * rows_dev, rows_dev)], kv.at[to], sems.at[half])
        )
        copies[-1].start()
    return copies


def own_stats_kernel(per_device, lengths, chip_any, q_ref, g_ref, stats_ref, kv, q_t, g_t, sems):
    core = lax.rem(lax.axis_index("dp"), 2)
    for copy in load_chip(chip_any, kv, sems, per_device * TILE, core):
        copy.wait()

    def unit(index, _):
        place = Place(lengths, per_device, index)
        turn_rows(place, q_ref, g_ref, q_t, g_t)

        def step(block, blocks, state):
            at = tiles(place.own_base + block, blocks)
            return tuple(
                gathered(state[head], *products(place, kv, at, q_t, g_t, head))[0] for head in range(HG)
            )

        zero = jnp.zeros((1, TILE), F32)
        start = tuple((jnp.full((1, TILE), -jnp.inf, F32), zero, zero) for _ in range(HG))
        state = sweep(place.own_count, OWN_STEPS, step, start)
        for head in range(HG):
            for row in range(3):
                stats_ref[place.slot + head, row : row + 1] = state[head][row]
        return 0

    lax.fori_loop(0, per_device * GROUPS, unit, 0)


def far_kernel(
    per_device, lengths, mine_0, mine_1, mine_2, twin_0, twin_1, twin_2, q_ref, g_ref, stats_in,
    dq_ref, stats_ref, mine_out_0, mine_out_1, mine_out_2, twin_out_0, twin_out_1, twin_out_2, kv, acc, low, exps, gprobs, maxes, keys_t, q_t, g_t, in_sems, out_sems,
):
    rows_dev = per_device * TILE
    me = lax.axis_index("dp")
    core = lax.rem(me, 2)
    column = lax.rem(me // 2, 2)

    def near(number, carrier, which):
        steps = [chip_step(relation, column) for relation in ROUNDS[number]]
        step = jnp.where(carrier == 0, steps[0], steps[1])
        chip = jnp.where(step < 0, step + REACH, step + REACH - 1)
        return pl.ds(pl.multiple_of((chip * 2 + which) * rows_dev, rows_dev), rows_dev)

    def halves():
        for number in range(len(ROUNDS)):
            for half in range(2):
                at = pl.ds(half * rows_dev, rows_dev)
                yield number, half, at

    arrived = ((mine_0, mine_1, mine_2), (twin_0, twin_1, twin_2))
    leaving = ((mine_out_0, mine_out_1, mine_out_2), (twin_out_0, twin_out_1, twin_out_2))
    loads = []
    for number, half, at in halves():
        for side, carrier in enumerate((core, 1 - core)):
            source = arrived[side][number]
            which = carrier if half == 0 else 1 - carrier
            loads.append(
                pltpu.make_async_copy(
                    source.at[at], kv.at[near(number, carrier, which)], in_sems.at[side, number, half]
                )
            )
            loads[-1].start()
    acc[...] = jnp.zeros_like(acc)
    for load in loads:
        load.wait()

    def unit(index, _):
        place = Place(lengths, per_device, index)

        @pl.when(place.group == 0)
        def _():
            def turn(block, _):
                keys_t[:, tiles(block, 1)] = kv[tiles(place.far_base + block, 1), :HD].T
                return 0

            lax.fori_loop(0, place.far_count, turn, 0)

        turn_rows(place, q_ref, g_ref, q_t, g_t)

        def scores(block, blocks, state):
            at, here = tiles(place.far_base + block, blocks), tiles(block, blocks)
            done = []
            for head in range(HG):
                score, gprob = products(place, kv, at, q_t, g_t, head)
                gprobs[head, here] = gprob
                after, weight = gathered(state[head], score, gprob)
                exps[head, here] = weight
                maxes[head, block] = after[0]
                done.append(after)
            return tuple(done)

        start = tuple(
            tuple(stats_in[place.slot + head, row : row + 1] for row in range(3)) for head in range(HG)
        )
        state = sweep(place.far_count, FAR_STEPS, scores, start)
        stats = tuple((top, 1.0 / total, weighted / total) for top, total, weighted in state)
        for head in range(HG):
            top, total, weighted = state[head]
            stats_ref[place.slot + head, 0:1] = top * SCALE_LOG2 + jnp.log2(total)
            stats_ref[place.slot + head, 1:2] = weighted / total
            dq_ref[place.slot + head] = jnp.zeros((HD, TILE), F32)

        def grads(block, blocks, _):
            at, here = tiles(place.far_base + block, blocks), tiles(block, blocks)
            key_t = keys_t[:, here]
            for head in range(HG):
                top, inverse, delta = stats[head]
                factor = jnp.exp2((maxes[head, block] - top) * SCALE_LOG2) * inverse
                prob = exps[head, here] * factor
                dscore = (prob * (gprobs[head, here] - delta)).astype(BF16)
                prob = prob.astype(BF16)
                dq_ref[place.slot + head] += jnp.dot(key_t, dscore, preferred_element_type=F32)
                acc[at, :HD] += SCALE * jnp.dot(
                    dscore, q_ref[place.rows, place.cols(head)], preferred_element_type=F32
                )
                acc[at, HD:] += jnp.dot(prob, g_ref[place.rows, place.cols(head)], preferred_element_type=F32)
            return 0

        sweep(place.far_count, FAR_STEPS, grads, 0)
        return 0

    lax.fori_loop(0, per_device * GROUPS, unit, 0)

    low[...] = acc[...].astype(BF16)
    stores = []
    for number, half, at in halves():
        for side, carrier in enumerate((core, 1 - core)):
            out = leaving[side][number]
            which = carrier if half == 0 else 1 - carrier
            stores.append(
                pltpu.make_async_copy(
                    low.at[near(number, carrier, which)], out.at[at], out_sems.at[side, number, half]
                )
            )
            stores[-1].start()
    for store in stores:
        store.wait()


def own_grads_kernel(
    per_device, lengths, chip_any, q_ref, g_ref, stats_ref, dq_in, dq_ref, own_out,
    kv, acc, keys_t, q_t, g_t, dq_t, sems, out_sems,
):
    rows_dev = per_device * TILE
    core = lax.rem(lax.axis_index("dp"), 2)
    loads = load_chip(chip_any, kv, sems, rows_dev, core)
    acc[...] = jnp.zeros_like(acc)
    for load in loads:
        load.wait()
    for block in range(2 * per_device):
        keys_t[block] = kv[block * TILE : (block + 1) * TILE, :HD].T

    def unit(index, _):
        place = Place(lengths, per_device, index)
        turn_rows(place, q_ref, g_ref, q_t, g_t)
        for head in range(HG):
            dq_t[head] = dq_in[place.slot + head]

        def grads(block, blocks, _):
            at = tiles(place.own_base + block, blocks)
            for head in range(HG):
                score, gprob = products(place, kv, at, q_t, g_t, head)
                prob = jnp.exp2(score * SCALE_LOG2 - stats_ref[place.slot + head, 0:1])
                dscore = (prob * (gprob - stats_ref[place.slot + head, 1:2])).astype(BF16)
                prob = prob.astype(BF16)
                dq = dq_t[head]
                for turn in range(blocks):
                    dq = dq + jnp.dot(
                        keys_t[place.own_base + block + turn],
                        dscore[turn * TILE : (turn + 1) * TILE],
                        preferred_element_type=F32,
                    )
                dq_t[head] = dq
                acc[at, :HD] += SCALE * jnp.dot(
                    dscore, q_ref[place.rows, place.cols(head)], preferred_element_type=F32
                )
                acc[at, HD:] += jnp.dot(prob, g_ref[place.rows, place.cols(head)], preferred_element_type=F32)
            return 0

        sweep(place.own_count, OWN_STEPS, grads, 0)
        for head in range(HG):
            dq_ref[place.rows, place.cols(head)] = (dq_t[head] * SCALE).T.astype(BF16)
        return 0

    lax.fori_loop(0, per_device * GROUPS, unit, 0)
    stores = []
    for half, which in enumerate((core, 1 - core)):
        source = pl.ds(pl.multiple_of(which * rows_dev, rows_dev), rows_dev)
        stores.append(
            pltpu.make_async_copy(acc.at[source], own_out.at[pl.ds(half * rows_dev, rows_dev)], out_sems.at[half])
        )
        stores[-1].start()
    for store in stores:
        store.wait()


def body(queries, kv_cache, grad_out, pair_lengths):
    rows_dev = queries.shape[0]
    per_device = rows_dev // TILE
    assert 2 * per_device * REACH >= MOST - 1
    count = lax.axis_size("dp")
    chip_rows = 2 * rows_dev
    far_rows = 2 * REACH * chip_rows
    slots = per_device * QH

    def send(value, number, back):
        pairs = []
        for source in range(count):
            row, column, core = source // 4, (source // 2) % 2, source % 2
            relation = ROUNDS[number][core]
            rows, across = {
                "row": (0, 1),
                "up": (1, 0),
                "down": (-1, 0),
                "up_across": (1, 1),
                "down_across": (-1, 1),
                "two_rows": (4 * column - 2, 1),
            }[relation]
            if back and relation != "two_rows":
                rows = -rows
            if 0 <= row + rows < count // 4:
                pairs.append((source, (row + rows) * 4 + (column ^ across) * 2 + core))
        return lax.ppermute(value, "dp", pairs)

    def to_twin(value):
        return lax.ppermute(value, "dp", [(i, i ^ 1) for i in range(count)])

    vmem = pl.BlockSpec(memory_space=pltpu.VMEM)
    hbm = pl.BlockSpec(memory_space=pl.ANY)
    smem = pl.BlockSpec(memory_space=pltpu.SMEM)
    turned = pltpu.VMEM((HG, HD, TILE), BF16)
    stats_shape = jax.ShapeDtypeStruct((slots, 8, TILE), F32)
    product = 2 * QH * TILE * TILE * HD * per_device

    def cost(products_done):
        return pl.CostEstimate(flops=3 * products_done * product, bytes_accessed=2**23, transcendentals=0)

    chip = jnp.concatenate([kv_cache, to_twin(kv_cache)], axis=0)
    arrived = [send(chip, number, True) for number in range(len(ROUNDS))]
    own_stats = pl.pallas_call(
        functools.partial(own_stats_kernel, per_device),
        out_shape=stats_shape,
        in_specs=[smem, hbm, vmem, vmem],
        out_specs=vmem,
        scratch_shapes=[pltpu.VMEM((chip_rows, 2 * HD), BF16), turned, turned, pltpu.SemaphoreType.DMA((2,))],
        compiler_params=pltpu.CompilerParams(vmem_limit_bytes=24 * 2**20),
        cost_estimate=cost(8),
        name="own_stats",
    )(pair_lengths, chip, queries, grad_out)

    arrived = [lax.optimization_barrier((rows, own_stats))[0] for rows in arrived]
    passed = jax.ShapeDtypeStruct((chip_rows, 2 * HD), BF16)
    dq_far, stats, *partial = pl.pallas_call(
        functools.partial(far_kernel, per_device),
        out_shape=(jax.ShapeDtypeStruct((slots, HD, TILE), F32), stats_shape) + (passed,) * 6,
        in_specs=[smem] + [hbm] * 6 + [vmem, vmem, vmem],
        out_specs=(vmem, vmem) + (hbm,) * 6,
        scratch_shapes=[
            pltpu.VMEM((far_rows, 2 * HD), BF16),
            pltpu.VMEM((far_rows, 2 * HD), F32),
            pltpu.VMEM((far_rows, 2 * HD), BF16),
            pltpu.VMEM((HG, (MOST - 1) * TILE, TILE), F32),
            pltpu.VMEM((HG, (MOST - 1) * TILE, TILE), F32),
            pltpu.VMEM((HG, MOST, 1, TILE), F32),
            pltpu.VMEM((HD, MOST * TILE), BF16),
            turned,
            turned,
            pltpu.SemaphoreType.DMA((2, len(ROUNDS), 2)),
            pltpu.SemaphoreType.DMA((2, len(ROUNDS), 2)),
        ],
        compiler_params=pltpu.CompilerParams(vmem_limit_bytes=44 * 2**20),
        cost_estimate=cost(40),
        name="far",
    )(pair_lengths, *arrived, *[to_twin(rows) for rows in arrived], queries, grad_out, own_stats)

    landed = []
    for number in range(len(ROUNDS)):
        both = partial[number].astype(F32) + to_twin(partial[len(ROUNDS) + number]).astype(F32)
        landed.append(send(both.astype(BF16), number, False))
    grad_queries, own_grad = pl.pallas_call(
        functools.partial(own_grads_kernel, per_device),
        out_shape=(
            jax.ShapeDtypeStruct(queries.shape, BF16),
            jax.ShapeDtypeStruct((chip_rows, 2 * HD), F32),
        ),
        in_specs=[smem, hbm, vmem, vmem, vmem, vmem],
        out_specs=(vmem, hbm),
        scratch_shapes=[
            pltpu.VMEM((chip_rows, 2 * HD), BF16),
            pltpu.VMEM((chip_rows, 2 * HD), F32),
            pltpu.VMEM((2 * per_device, HD, TILE), BF16),
            turned,
            turned,
            pltpu.VMEM((HG, HD, TILE), F32),
            pltpu.SemaphoreType.DMA((2,)),
            pltpu.SemaphoreType.DMA((2,)),
        ],
        compiler_params=pltpu.CompilerParams(vmem_limit_bytes=32 * 2**20),
        cost_estimate=cost(20),
        name="own_grads",
    )(pair_lengths, chip, queries, grad_out, stats, dq_far)
    total = own_grad
    for part in landed:
        total = total + part.astype(F32)
    grad_kv = total[:rows_dev] + to_twin(total[rows_dev:].astype(BF16)).astype(F32)
    return grad_queries, grad_kv


def solution(mesh):
    tokens = P(("groups", "dp"), None)
    return jax.shard_map(
        body,
        mesh=mesh,
        in_specs=(tokens, tokens, tokens, P("groups")),
        out_specs=(tokens, tokens),
        check_vma=False,
    )
```

profile of v0, /device:TPU:9, one launch (start us, length us, event | category | flops | bytes accessed | tf_op | source)
XLA Modules:
  0.0 109.5 jit_solution(13466273363858093227)
XLA Ops:
  0.6 0.7 collective-permute-start
  1.4 1.0 constant_dynamic-update-slice_fusion.1
  2.3 0.4 collective-permute-done
  2.7 0.0 copy-start.5
  2.8 3.2 %collective-permute-start.3 = (bf16[1024,256]{1,0:T(8,128)(2,1)S(1)}, bf16[1024,256]{1,0:T(8,128)(2,1)S(1)}, u32[]{:S(2)}, u32[]{:S(2)}) collective-permute-start(bf16[1024,256]{1,0:T(8,128)(2,1)S(1)} %constant_dynamic-update-slice_fusion.chip_any), channel_id=1, source_target_pairs={{1,5},{3,7},{4,0},{5,9},{6,2},{7,11},{8,4},{9,13},{10,6},{11,15},{... | collective-permute-start | bytes 1572872 | tf_op jit(solution)/shard_map/ppermute | solution.py:335
  6.0 4.2 %collective-permute-start.2 = (bf16[1024,256]{1,0:T(8,128)(2,1)S(1)}, bf16[1024,256]{1,0:T(8,128)(2,1)S(1)}, u32[]{:S(2)}, u32[]{:S(2)}) collective-permute-start(bf16[1024,256]{1,0:T(8,128)(2,1)S(1)} %constant_dynamic-update-slice_fusion.chip_any), channel_id=1, source_target_pairs={{1,7},{3,5},{4,2},{5,11},{6,0},{7,9},{8,6},{9,15},{10,4},{11,13},{... | collective-permute-start | bytes 1572872 | tf_op jit(solution)/shard_map/ppermute | solution.py:335
  10.1 0.7 collective-permute-start.1
  10.8 0.0 copy-start
  10.9 1.2 %copy-done = bf16[512,1024]{1,0:T(8,128)(2,1)S(1)} copy-done((bf16[512,1024]{1,0:T(8,128)(2,1)S(1)}, bf16[512,1024]{1,0:T(8,128)(2,1)}, u32[]{:S(2)}) %copy-start) | copy-done | bytes 1048600
  12.1 1.2 %copy-done.2 = bf16[512,1024]{1,0:T(8,128)(2,1)S(1)} copy-done((bf16[512,1024]{1,0:T(8,128)(2,1)S(1)}, bf16[512,1024]{1,0:T(8,128)(2,1)}, u32[]{:S(2)}) %copy-start.2) | copy-done | bytes 1048600
  13.3 0.0 copy-start.4
  13.3 0.7 copy-done.4
  14.0 0.0 copy-start.1
  14.0 7.6 %own_stats.1.stats_in = f32[16,8,256]{2,1,0:T(8,128)S(1)} custom-call(s32[10]{0:T(128)S(1)} %copy-done.4, bf16[1024,256]{1,0:T(8,128)(2,1)S(1)} %constant_dynamic-update-slice_fusion.chip_any, bf16[512,1024]{1,0:T(8,128)(2,1)S(1)} %copy-done, bf16[512,1024]{1,0:T(8,128)(2,1)S(1)} %copy-done.2), custom_call_target="tpu_custom_call" | custom-call | flops 6442450944 | bytes 8388608 | tf_op jit(solution)/shard_map/own_stats/pallas_call | solution.py:352
  21.6 0.0 collective-permute-done.3.mine_2
  21.6 0.1 collective-permute-start.6
  21.7 2.5 %collective-permute-done.2.mine_1 = bf16[1024,256]{1,0:T(8,128)(2,1)S(1)} collective-permute-done((bf16[1024,256]{1,0:T(8,128)(2,1)S(1)}, bf16[1024,256]{1,0:T(8,128)(2,1)S(1)}, u32[]{:S(2)}, u32[]{:S(2)}) %collective-permute-start.2) | collective-permute-done | bytes 524320 | tf_op jit(solution)/shard_map/ppermute | solution.py:335
  24.1 1.5 %collective-permute-start.5 = (bf16[1024,256]{1,0:T(8,128)(2,1)S(1)}, bf16[1024,256]{1,0:T(8,128)(2,1)S(1)}, u32[]{:S(2)}, u32[]{:S(2)}) collective-permute-start(bf16[1024,256]{1,0:T(8,128)(2,1)S(1)} %collective-permute-done.2.mine_1), channel_id=1, source_target_pairs={{0,1},{1,0},{2,3},{3,2},{4,5},{5,4},{6,7},{7,6},{8,9},{9,8},{10,11... | collective-permute-start | bytes 1572872 | tf_op jit(solution)/shard_map/ppermute | solution.py:338
  25.7 0.0 collective-permute-done.1.mine_0
  25.7 8.7 %collective-permute-start.4 = (bf16[1024,256]{1,0:T(8,128)(2,1)S(1)}, bf16[1024,256]{1,0:T(8,128)(2,1)S(1)}, u32[]{:S(2)}, u32[]{:S(2)}) collective-permute-start(bf16[1024,256]{1,0:T(8,128)(2,1)S(1)} %collective-permute-done.1.mine_0), channel_id=1, source_target_pairs={{0,1},{1,0},{2,3},{3,2},{4,5},{5,4},{6,7},{7,6},{8,9},{9,8},{10,11... | collective-permute-start | bytes 1572872 | tf_op jit(solution)/shard_map/ppermute | solution.py:338
  34.4 0.0 collective-permute-done.6.twin_2
  34.4 0.0 collective-permute-done.5.twin_1
  34.4 1.5 %collective-permute-done.4.twin_0 = bf16[1024,256]{1,0:T(8,128)(2,1)S(1)} collective-permute-done((bf16[1024,256]{1,0:T(8,128)(2,1)S(1)}, bf16[1024,256]{1,0:T(8,128)(2,1)S(1)}, u32[]{:S(2)}, u32[]{:S(2)}) %collective-permute-start.4) | collective-permute-done | bytes 524320 | tf_op jit(solution)/shard_map/ppermute | solution.py:338
  35.9 0.0 copy-done.5
  35.9 0.0 copy-done.1
  35.9 0.0 copy-done.3
  35.9 9.3 %far.1 = (f32[16,128,256]{2,1,0:T(8,128)}, f32[16,8,256]{2,1,0:T(8,128)S(1)}, bf16[1024,256]{1,0:T(8,128)(2,1)S(1)}, bf16[1024,256]{1,0:T(8,128)(2,1)S(1)}, bf16...) custom-call(s32[10]{0:T(128)S(1)} %copy-done.5, ...), custom_call_target="tpu_custom_call" | custom-call | flops 32212254720 | bytes 8388608 | tf_op jit(solution)/shard_map/far/pallas_call | solution.py:365
  45.3 2.2 %collective-permute-start.7 = (bf16[1024,256]{1,0:T(8,128)(2,1)S(1)}, bf16[1024,256]{1,0:T(8,128)(2,1)S(1)}, u32[]{:S(2)}, u32[]{:S(2)}) collective-permute-start(bf16[1024,256]{1,0:T(8,128)(2,1)S(1)} %get-tuple-element.23), channel_id=1, source_target_pairs={{0,1},{1,0},{2,3},{3,2},{4,5},{5,4},{6,7},{7,6},{8,9},{9,8},{10,11... | collective-permute-start | bytes 1572872 | tf_op jit(solution)/shard_map/ppermute | solution.py:338
  47.5 0.1 collective-permute-start.9
  47.5 0.4 collective-permute-start.11
  48.0 1.0 collective-permute-done.7
  49.0 0.1 add_convert_fusion.2
  49.1 0.8 collective-permute-start.8
  50.0 0.0 collective-permute-done.9
  50.0 0.1 add_convert_fusion.1
  50.1 32.1 %collective-permute-start.10 = (bf16[1024,256]{1,0:T(8,128)(2,1)S(1)}, bf16[1024,256]{1,0:T(8,128)(2,1)S(1)}, u32[]{:S(2)}, u32[]{:S(2)}) collective-permute-start(bf16[1024,256]{1,0:T(8,128)(2,1)S(1)} %add_convert_fusion.1), channel_id=1, source_target_pairs={{0,6},{2,4},{4,10},{5,3},{6,8},{7,1},{8,14},{9,7},{10,12},{11,5},{... | collective-permute-start | bytes 1572872 | tf_op jit(solution)/shard_map/ppermute | solution.py:335
  82.2 0.0 collective-permute-done.11
  82.2 0.1 add_convert_fusion
  82.4 1.9 %collective-permute-start.12 = (bf16[1024,256]{1,0:T(8,128)(2,1)S(1)}, bf16[1024,256]{1,0:T(8,128)(2,1)S(1)}, u32[]{:S(2)}, u32[]{:S(2)}) collective-permute-start(bf16[1024,256]{1,0:T(8,128)(2,1)S(1)} %add_convert_fusion), channel_id=1, source_target_pairs={{0,4},{2,6},{4,8},{5,1},{6,10},{7,3},{8,12},{9,5},{10,14},{11,7},{... | collective-permute-start | bytes 1572872 | tf_op jit(solution)/shard_map/ppermute | solution.py:335
  84.3 0.0 copy-done.6
  84.3 16.4 %own_grads.1 = (bf16[512,1024]{1,0:T(8,128)(2,1)}, f32[1024,256]{1,0:T(8,128)S(1)}) custom-call(s32[10]{0:T(128)S(1)} %copy-done.5, bf16[1024,256]{1,0:T(8,128)(2,1)S(1)} %constant_dynamic-update-slice_fusion.chip_any, bf16[512,1024]{1,0:T(8,128)(2,1)S(1)} %copy-done.1, bf16[512,1024]{1,0:T(8,128)(2,1)S(1)} %copy-done.3, ...), custom_call_target="tpu_custom_call" | custom-call | flops 16106127360 | bytes 8388608 | tf_op jit(solution)/shard_map/own_grads/pallas_call | solution.py:392
  100.7 0.0 collective-permute-done.8
  100.7 0.0 collective-permute-done.10
  100.7 6.1 %collective-permute-done.12 = bf16[1024,256]{1,0:T(8,128)(2,1)S(1)} collective-permute-done((bf16[1024,256]{1,0:T(8,128)(2,1)S(1)}, bf16[1024,256]{1,0:T(8,128)(2,1)S(1)}, u32[]{:S(2)}, u32[]{:S(2)}) %collective-permute-start.12) | collective-permute-done | bytes 524320 | tf_op jit(solution)/shard_map/ppermute | solution.py:335
  106.8 0.2 convert_add_fusion
  107.1 0.1 collective-permute-start.13
  107.1 1.5 %collective-permute-done.13 = bf16[512,256]{1,0:T(8,128)(2,1)S(1)} collective-permute-done((bf16[512,256]{1,0:T(8,128)(2,1)S(1)}, bf16[512,256]{1,0:T(8,128)(2,1)S(1)}, u32[]{:S(2)}, u32[]{:S(2)}) %collective-permute-start.13) | collective-permute-done | bytes 262176 | tf_op jit(solution)/shard_map/ppermute | solution.py:338
  108.7 0.8 slice_add_fusion
  (5 shorter events, 0.1 us)
Async XLA Ops:
  0.6 2.1 %collective-permute-start = (bf16[512,256]{1,0:T(8,128)(2,1)}, bf16[512,256]{1,0:T(8,128)(2,1)S(1)}, u32[]{:S(2)}, u32[]{:S(2)}) collective-permute-start(bf16[512,256]{1,0:T(8,128)(2,1)} %param.5), channel_id=1, source_target_pairs={{0,1},{1,0},{2,3},{3,2},{4,5},{5,4},{6,7},{7,6},{8,9},{9,8},{10,11... | collective-permute-start | bytes 786440 | tf_op jit(solution)/shard_map/ppermute | solution.py:338
  2.7 33.2 %copy-start.5 = (s32[10]{0:T(128)S(1)}, s32[10]{0:T(128)}, u32[]{:S(2)}) copy-start(s32[10]{0:T(128)} %lengths.5) | copy-start | bytes 124
  2.8 18.8 %collective-permute-start.3 = (bf16[1024,256]{1,0:T(8,128)(2,1)S(1)}, bf16[1024,256]{1,0:T(8,128)(2,1)S(1)}, u32[]{:S(2)}, u32[]{:S(2)}) collective-permute-start(bf16[1024,256]{1,0:T(8,128)(2,1)S(1)} %constant_dynamic-update-slice_fusion.chip_any), channel_id=1, source_target_pairs={{1,5},{3,7},{4,0},{5,9},{6,2},{7,11},{8,4},{9,13},{10,6},{11,15},{... | collective-permute-start | bytes 1572872 | tf_op jit(solution)/shard_map/ppermute | solution.py:335
  6.0 18.2 %collective-permute-start.2 = (bf16[1024,256]{1,0:T(8,128)(2,1)S(1)}, bf16[1024,256]{1,0:T(8,128)(2,1)S(1)}, u32[]{:S(2)}, u32[]{:S(2)}) collective-permute-start(bf16[1024,256]{1,0:T(8,128)(2,1)S(1)} %constant_dynamic-update-slice_fusion.chip_any), channel_id=1, source_target_pairs={{1,7},{3,5},{4,2},{5,11},{6,0},{7,9},{8,6},{9,15},{10,4},{11,13},{... | collective-permute-start | bytes 1572872 | tf_op jit(solution)/shard_map/ppermute | solution.py:335
  10.1 15.5 %collective-permute-start.1 = (bf16[1024,256]{1,0:T(8,128)(2,1)S(1)}, bf16[1024,256]{1,0:T(8,128)(2,1)S(1)}, u32[]{:S(2)}, u32[]{:S(2)}) collective-permute-start(bf16[1024,256]{1,0:T(8,128)(2,1)S(1)} %constant_dynamic-update-slice_fusion.chip_any), channel_id=1, source_target_pairs={{0,2},{2,0},{3,9},{4,6},{6,4},{7,13},{8,10},{9,3},{10,8},{12,14},{... | collective-permute-start | bytes 1572872 | tf_op jit(solution)/shard_map/ppermute | solution.py:335
  10.8 1.2 %copy-start = (bf16[512,1024]{1,0:T(8,128)(2,1)S(1)}, bf16[512,1024]{1,0:T(8,128)(2,1)}, u32[]{:S(2)}) copy-start(bf16[512,1024]{1,0:T(8,128)(2,1)} %q_ref.5) | copy-start | bytes 3145732
  12.1 1.2 %copy-start.2 = (bf16[512,1024]{1,0:T(8,128)(2,1)S(1)}, bf16[512,1024]{1,0:T(8,128)(2,1)}, u32[]{:S(2)}) copy-start(bf16[512,1024]{1,0:T(8,128)(2,1)} %g_ref.5) | copy-start | bytes 3145732
  13.3 0.7 copy-start.4
  14.0 22.0 %copy-start.1 = (bf16[512,1024]{1,0:T(8,128)(2,1)S(1)}, bf16[512,1024]{1,0:T(8,128)(2,1)}, u32[]{:S(2)}) copy-start(bf16[512,1024]{1,0:T(8,128)(2,1)} %q_ref.5) | copy-start | bytes 3145732
  14.0 22.0 %copy-start.3 = (bf16[512,1024]{1,0:T(8,128)(2,1)S(1)}, bf16[512,1024]{1,0:T(8,128)(2,1)}, u32[]{:S(2)}) copy-start(bf16[512,1024]{1,0:T(8,128)(2,1)} %g_ref.5) | copy-start | bytes 3145732
  21.6 12.8 %collective-permute-start.6 = (bf16[1024,256]{1,0:T(8,128)(2,1)S(1)}, bf16[1024,256]{1,0:T(8,128)(2,1)S(1)}, u32[]{:S(2)}, u32[]{:S(2)}) collective-permute-start(bf16[1024,256]{1,0:T(8,128)(2,1)S(1)} %collective-permute-done.3.mine_2), channel_id=1, source_target_pairs={{0,1},{1,0},{2,3},{3,2},{4,5},{5,4},{6,7},{7,6},{8,9},{9,8},{10,11... | collective-permute-start | bytes 1572872 | tf_op jit(solution)/shard_map/ppermute | solution.py:338
  24.1 10.3 %collective-permute-start.5 = (bf16[1024,256]{1,0:T(8,128)(2,1)S(1)}, bf16[1024,256]{1,0:T(8,128)(2,1)S(1)}, u32[]{:S(2)}, u32[]{:S(2)}) collective-permute-start(bf16[1024,256]{1,0:T(8,128)(2,1)S(1)} %collective-permute-done.2.mine_1), channel_id=1, source_target_pairs={{0,1},{1,0},{2,3},{3,2},{4,5},{5,4},{6,7},{7,6},{8,9},{9,8},{10,11... | collective-permute-start | bytes 1572872 | tf_op jit(solution)/shard_map/ppermute | solution.py:338
  25.7 10.3 %collective-permute-start.4 = (bf16[1024,256]{1,0:T(8,128)(2,1)S(1)}, bf16[1024,256]{1,0:T(8,128)(2,1)S(1)}, u32[]{:S(2)}, u32[]{:S(2)}) collective-permute-start(bf16[1024,256]{1,0:T(8,128)(2,1)S(1)} %collective-permute-done.1.mine_0), channel_id=1, source_target_pairs={{0,1},{1,0},{2,3},{3,2},{4,5},{5,4},{6,7},{7,6},{8,9},{9,8},{10,11... | collective-permute-start | bytes 1572872 | tf_op jit(solution)/shard_map/ppermute | solution.py:338
  45.3 3.7 %collective-permute-start.7 = (bf16[1024,256]{1,0:T(8,128)(2,1)S(1)}, bf16[1024,256]{1,0:T(8,128)(2,1)S(1)}, u32[]{:S(2)}, u32[]{:S(2)}) collective-permute-start(bf16[1024,256]{1,0:T(8,128)(2,1)S(1)} %get-tuple-element.23), channel_id=1, source_target_pairs={{0,1},{1,0},{2,3},{3,2},{4,5},{5,4},{6,7},{7,6},{8,9},{9,8},{10,11... | collective-permute-start | bytes 1572872 | tf_op jit(solution)/shard_map/ppermute | solution.py:338
  47.5 2.5 %collective-permute-start.9 = (bf16[1024,256]{1,0:T(8,128)(2,1)S(1)}, bf16[1024,256]{1,0:T(8,128)(2,1)S(1)}, u32[]{:S(2)}, u32[]{:S(2)}) collective-permute-start(bf16[1024,256]{1,0:T(8,128)(2,1)S(1)} %get-tuple-element.25), channel_id=1, source_target_pairs={{0,1},{1,0},{2,3},{3,2},{4,5},{5,4},{6,7},{7,6},{8,9},{9,8},{10,11... | collective-permute-start | bytes 1572872 | tf_op jit(solution)/shard_map/ppermute | solution.py:338
  47.5 34.7 %collective-permute-start.11 = (bf16[1024,256]{1,0:T(8,128)(2,1)S(1)}, bf16[1024,256]{1,0:T(8,128)(2,1)S(1)}, u32[]{:S(2)}, u32[]{:S(2)}) collective-permute-start(bf16[1024,256]{1,0:T(8,128)(2,1)S(1)} %get-tuple-element.27), channel_id=1, source_target_pairs={{0,1},{1,0},{2,3},{3,2},{4,5},{5,4},{6,7},{7,6},{8,9},{9,8},{10,11... | collective-permute-start | bytes 1572872 | tf_op jit(solution)/shard_map/ppermute | solution.py:338
  49.0 35.3 %copy-start.6 = (f32[16,128,256]{2,1,0:T(8,128)S(1)}, f32[16,128,256]{2,1,0:T(8,128)}, u32[]{:S(2)}) copy-start(f32[16,128,256]{2,1,0:T(8,128)} %get-tuple-element.19.dq_in) | copy-start | bytes 6291460
  49.1 51.6 %collective-permute-start.8 = (bf16[1024,256]{1,0:T(8,128)(2,1)S(1)}, bf16[1024,256]{1,0:T(8,128)(2,1)S(1)}, u32[]{:S(2)}, u32[]{:S(2)}) collective-permute-start(bf16[1024,256]{1,0:T(8,128)(2,1)S(1)} %add_convert_fusion.2), channel_id=1, source_target_pairs={{0,2},{2,0},{3,9},{4,6},{6,4},{7,13},{8,10},{9,3},{10,8},{12,14},{... | collective-permute-start | bytes 1572872 | tf_op jit(solution)/shard_map/ppermute | solution.py:335
  50.1 50.6 %collective-permute-start.10 = (bf16[1024,256]{1,0:T(8,128)(2,1)S(1)}, bf16[1024,256]{1,0:T(8,128)(2,1)S(1)}, u32[]{:S(2)}, u32[]{:S(2)}) collective-permute-start(bf16[1024,256]{1,0:T(8,128)(2,1)S(1)} %add_convert_fusion.1), channel_id=1, source_target_pairs={{0,6},{2,4},{4,10},{5,3},{6,8},{7,1},{8,14},{9,7},{10,12},{11,5},{... | collective-permute-start | bytes 1572872 | tf_op jit(solution)/shard_map/ppermute | solution.py:335
  82.4 24.5 %collective-permute-start.12 = (bf16[1024,256]{1,0:T(8,128)(2,1)S(1)}, bf16[1024,256]{1,0:T(8,128)(2,1)S(1)}, u32[]{:S(2)}, u32[]{:S(2)}) collective-permute-start(bf16[1024,256]{1,0:T(8,128)(2,1)S(1)} %add_convert_fusion), channel_id=1, source_target_pairs={{0,4},{2,6},{4,8},{5,1},{6,10},{7,3},{8,12},{9,5},{10,14},{11,7},{... | collective-permute-start | bytes 1572872 | tf_op jit(solution)/shard_map/ppermute | solution.py:335
  107.1 1.6 %collective-permute-start.13 = (bf16[512,256]{1,0:T(8,128)(2,1)S(1)}, bf16[512,256]{1,0:T(8,128)(2,1)S(1)}, u32[]{:S(2)}, u32[]{:S(2)}) collective-permute-start(bf16[512,256]{1,0:T(8,128)(2,1)S(1)} %slice.13), channel_id=1, source_target_pairs={{0,1},{1,0},{2,3},{3,2},{4,5},{5,4},{6,7},{7,6},{8,9},{9,8},{10,11... | collective-permute-start | bytes 786440 | tf_op jit(solution)/shard_map/ppermute | solution.py:338
where the time goes:
time: 110 us
  starting transfers between devices  56.7 us (52%)
  Pallas kernels  33.3 us (30%)
  waiting for transfers between devices  13.1 us (12%)
  local copies, waits for them, and re-layouts  4.13 us (4%)
  other arithmetic  1.47 us (1%)
    ppermute x6, starting transfers between devices, send(): return lax.ppermute(value, 'dp', pairs)  42.9 us
    pallas_call x1, Pallas kernels, body(): pl.pallas_call(functools.partial(own_grads_kernel, per_device), out_shape...  16.4 us
    ppermute x8, starting transfers between devices, to_twin(): return lax.ppermute(value, 'dp', [(i, i ^ 1) for i in range(count)])  13.8 us
    pallas_call x1, Pallas kernels, body(): pl.pallas_call(functools.partial(far_kernel, per_device), out_shape=(jax....  9.32 us
    ppermute x6, waiting for transfers between devices, send(): return lax.ppermute(value, 'dp', pairs)  8.57 us
    pallas_call x1, Pallas kernels, body(): pl.pallas_call(functools.partial(own_stats_kernel, per_device), out_shape...  7.61 us
    ppermute x8, waiting for transfers between devices, to_twin(): return lax.ppermute(value, 'dp', [(i, i ^ 1) for i in range(count)])  4.49 us
    unnamed x15, local copies, waits for them, and re-layouts  4.08 us
  transfers between devices with their start and end apart: 14, of which 6 were waited for; matrix products, arithmetic and copies ran while one was open for 1% of the time, Pallas kernels for 22%

commit v1 on v0

--- a/solution.py
+++ b/solution.py
@@ -21,7 +21,8 @@
 BF16 = jnp.bfloat16
 GROUPS = QH // HG
 
-ROUNDS = (("row", "two_rows"), ("up_across", "down_across"), ("up", "down"))
+ROUNDS = (("row", "near_across"), ("far_across", "two_rows"), ("up", "down"))
+SHORT = 1
 
 
 def chip_step(relation, column):
@@ -29,9 +30,20 @@
         "row": 1 - 2 * column,
         "up": 2,
         "down": -2,
-        "up_across": 3 - 2 * column,
-        "down_across": -1 - 2 * column,
+        "near_across": 2 * column - 1,
+        "far_across": 3 - 6 * column,
         "two_rows": 6 * column - 3,
+    }[relation]
+
+
+def grid_step(relation, column):
+    return {
+        "row": (0, 1),
+        "up": (1, 0),
+        "down": (-1, 0),
+        "near_across": (2 * column - 1, 1),
+        "far_across": (1 - 2 * column, 1),
+        "two_rows": (4 * column - 2, 1),
     }[relation]
 
 
@@ -101,22 +113,7 @@
         g_t[head] = g_ref[place.rows, place.cols(head)].T
 
 
-def load_chip(chip_any, kv, sems, rows_dev, core):
-    copies = []
-    for half, which in enumerate((core, 1 - core)):
-        to = pl.ds(pl.multiple_of(which * rows_dev, rows_dev), rows_dev)
-        copies.append(
-            pltpu.make_async_copy(chip_any.at[pl.ds(half * rows_dev, rows_dev)], kv.at[to], sems.at[half])
-        )
-        copies[-1].start()
-    return copies
-
-
-def own_stats_kernel(per_device, lengths, chip_any, q_ref, g_ref, stats_ref, kv, q_t, g_t, sems):
-    core = lax.rem(lax.axis_index("dp"), 2)
-    for copy in load_chip(chip_any, kv, sems, per_device * TILE, core):
-        copy.wait()
-
+def own_stats_kernel(per_device, lengths, kv, q_ref, g_ref, stats_ref, q_t, g_t):
     def unit(index, _):
         place = Place(lengths, per_device, index)
         turn_rows(place, q_ref, g_ref, q_t, g_t)
@@ -140,35 +137,29 @@
 
 def far_kernel(
     per_device, lengths, mine_0, mine_1, mine_2, twin_0, twin_1, twin_2, q_ref, g_ref, stats_in,
-    dq_ref, stats_ref, mine_out_0, mine_out_1, mine_out_2, twin_out_0, twin_out_1, twin_out_2, kv, acc, low, exps, gprobs, maxes, keys_t, q_t, g_t, in_sems, out_sems,
+    dq_out, stats_ref, mine_out_0, mine_out_1, mine_out_2, twin_out_0, twin_out_1, twin_out_2, kv, acc, low, exps, gprobs, maxes, keys_t, q_t, g_t, dq_ref, in_sems, out_sems, dq_sems,
 ):
-    rows_dev = per_device * TILE
+    per_chip = 2 * per_device
     me = lax.axis_index("dp")
     core = lax.rem(me, 2)
     column = lax.rem(me // 2, 2)
 
-    def near(number, carrier, which):
+    def near(number, carrier):
         steps = [chip_step(relation, column) for relation in ROUNDS[number]]
         step = jnp.where(carrier == 0, steps[0], steps[1])
-        chip = jnp.where(step < 0, step + REACH, step + REACH - 1)
-        return pl.ds(pl.multiple_of((chip * 2 + which) * rows_dev, rows_dev), rows_dev)
-
-    def halves():
-        for number in range(len(ROUNDS)):
-            for half in range(2):
-                at = pl.ds(half * rows_dev, rows_dev)
-                yield number, half, at
+        tile = jnp.where(step < 0, step + REACH, step + REACH - 1) * per_chip
+        if number == SHORT:
+            return tiles(tile + jnp.where(step < 0, 1, 0), per_chip - 1)
+        return tiles(tile, per_chip)
 
     arrived = ((mine_0, mine_1, mine_2), (twin_0, twin_1, twin_2))
     leaving = ((mine_out_0, mine_out_1, mine_out_2), (twin_out_0, twin_out_1, twin_out_2))
     loads = []
-    for number, half, at in halves():
+    for number in range(len(ROUNDS)):
         for side, carrier in enumerate((core, 1 - core)):
-            source = arrived[side][number]
-            which = carrier if half == 0 else 1 - carrier
             loads.append(
                 pltpu.make_async_copy(
-                    source.at[at], kv.at[near(number, carrier, which)], in_sems.at[side, number, half]
+                    arrived[side][number], kv.at[near(number, carrier)], in_sems.at[side, number]
                 )
             )
             loads[-1].start()
@@ -229,36 +220,35 @@
             return 0
 
         sweep(place.far_count, FAR_STEPS, grads, 0)
+        dq_copy(index).start()
         return 0
+
+    def dq_copy(index):
+        at = pl.ds(index * HG, HG)
+        return pltpu.make_async_copy(dq_ref.at[at], dq_out.at[at], dq_sems.at[index])
 
     lax.fori_loop(0, per_device * GROUPS, unit, 0)
 
     low[...] = acc[...].astype(BF16)
     stores = []
-    for number, half, at in halves():
+    for number in range(len(ROUNDS)):
         for side, carrier in enumerate((core, 1 - core)):
-            out = leaving[side][number]
-            which = carrier if half == 0 else 1 - carrier
             stores.append(
                 pltpu.make_async_copy(
-                    low.at[near(number, carrier, which)], out.at[at], out_sems.at[side, number, half]
+                    low.at[near(number, carrier)], leaving[side][number], out_sems.at[side, number]
                 )
             )
             stores[-1].start()
+    for index in range(per_device * GROUPS):
+        dq_copy(index).wait()
     for store in stores:
         store.wait()
 
 
 def own_grads_kernel(
-    per_device, lengths, chip_any, q_ref, g_ref, stats_ref, dq_in, dq_ref, own_out,
-    kv, acc, keys_t, q_t, g_t, dq_t, sems, out_sems,
+    per_device, lengths, kv, q_ref, g_ref, stats_ref, dq_in, dq_ref, acc, keys_t, q_t, g_t, dq_t
 ):
-    rows_dev = per_device * TILE
-    core = lax.rem(lax.axis_index("dp"), 2)
-    loads = load_chip(chip_any, kv, sems, rows_dev, core)
     acc[...] = jnp.zeros_like(acc)
-    for load in loads:
-        load.wait()
     for block in range(2 * per_device):
         keys_t[block] = kv[block * TILE : (block + 1) * TILE, :HD].T
 
@@ -295,21 +285,12 @@
         return 0
 
     lax.fori_loop(0, per_device * GROUPS, unit, 0)
-    stores = []
-    for half, which in enumerate((core, 1 - core)):
-        source = pl.ds(pl.multiple_of(which * rows_dev, rows_dev), rows_dev)
-        stores.append(
-            pltpu.make_async_copy(acc.at[source], own_out.at[pl.ds(half * rows_dev, rows_dev)], out_sems.at[half])
-        )
-        stores[-1].start()
-    for store in stores:
-        store.wait()
 
 
 def body(queries, kv_cache, grad_out, pair_lengths):
     rows_dev = queries.shape[0]
     per_device = rows_dev // TILE
-    assert 2 * per_device * REACH >= MOST - 1
+    assert 2 * per_device * REACH >= MOST
     count = lax.axis_size("dp")
     chip_rows = 2 * rows_dev
     far_rows = 2 * REACH * chip_rows
@@ -320,15 +301,8 @@
         for source in range(count):
             row, column, core = source // 4, (source // 2) % 2, source % 2
             relation = ROUNDS[number][core]
-            rows, across = {
-                "row": (0, 1),
-                "up": (1, 0),
-                "down": (-1, 0),
-                "up_across": (1, 1),
-                "down_across": (-1, 1),
-                "two_rows": (4 * column - 2, 1),
-            }[relation]
-            if back and relation != "two_rows":
+            rows, across = grid_step(relation, column)
+            if back and relation in ("up", "down"):
                 rows = -rows
             if 0 <= row + rows < count // 4:
                 pairs.append((source, (row + rows) * 4 + (column ^ across) * 2 + core))
@@ -347,26 +321,33 @@
     def cost(products_done):
         return pl.CostEstimate(flops=3 * products_done * product, bytes_accessed=2**23, transcendentals=0)
 
-    chip = jnp.concatenate([kv_cache, to_twin(kv_cache)], axis=0)
-    arrived = [send(chip, number, True) for number in range(len(ROUNDS))]
+    me = lax.axis_index("dp")
+    core, column = me & 1, (me >> 1) & 1
+    skipped = jnp.where(core == column, TILE, 0)
+    short_rows = chip_rows - TILE
+    chip = lax.dynamic_slice_in_dim(
+        jnp.concatenate([kv_cache, to_twin(kv_cache), kv_cache], axis=0), core * rows_dev, chip_rows, 0
+    )
+    short = lax.dynamic_slice_in_dim(chip, skipped, short_rows, 0)
+    arrived = [send(short if number == SHORT else chip, number, True) for number in range(len(ROUNDS))]
     own_stats = pl.pallas_call(
         functools.partial(own_stats_kernel, per_device),
         out_shape=stats_shape,
-        in_specs=[smem, hbm, vmem, vmem],
+        in_specs=[smem, vmem, vmem, vmem],
         out_specs=vmem,
-        scratch_shapes=[pltpu.VMEM((chip_rows, 2 * HD), BF16), turned, turned, pltpu.SemaphoreType.DMA((2,))],
+        scratch_shapes=[turned, turned],
         compiler_params=pltpu.CompilerParams(vmem_limit_bytes=24 * 2**20),
         cost_estimate=cost(8),
         name="own_stats",
     )(pair_lengths, chip, queries, grad_out)
 
     arrived = [lax.optimization_barrier((rows, own_stats))[0] for rows in arrived]
-    passed = jax.ShapeDtypeStruct((chip_rows, 2 * HD), BF16)
+    passed = tuple(jax.ShapeDtypeStruct(rows.shape, BF16) for rows in arrived)
     dq_far, stats, *partial = pl.pallas_call(
         functools.partial(far_kernel, per_device),
-        out_shape=(jax.ShapeDtypeStruct((slots, HD, TILE), F32), stats_shape) + (passed,) * 6,
+        out_shape=(pltpu.HBM((slots, HD, TILE), F32), stats_shape) + passed + passed,
         in_specs=[smem] + [hbm] * 6 + [vmem, vmem, vmem],
-        out_specs=(vmem, vmem) + (hbm,) * 6,
+        out_specs=(pl.BlockSpec(memory_space=pltpu.HBM), vmem) + (hbm,) * 6,
         scratch_shapes=[
             pltpu.VMEM((far_rows, 2 * HD), BF16),
             pltpu.VMEM((far_rows, 2 * HD), F32),
@@ -377,10 +358,12 @@
             pltpu.VMEM((HD, MOST * TILE), BF16),
             turned,
             turned,
-            pltpu.SemaphoreType.DMA((2, len(ROUNDS), 2)),
-            pltpu.SemaphoreType.DMA((2, len(ROUNDS), 2)),
+            pltpu.VMEM((slots, HD, TILE), F32),
+            pltpu.SemaphoreType.DMA((2, len(ROUNDS))),
+            pltpu.SemaphoreType.DMA((2, len(ROUNDS))),
+            pltpu.SemaphoreType.DMA((per_device * GROUPS,)),
         ],
-        compiler_params=pltpu.CompilerParams(vmem_limit_bytes=44 * 2**20),
+        compiler_params=pltpu.CompilerParams(vmem_limit_bytes=43 * 2**20),
         cost_estimate=cost(40),
         name="far",
     )(pair_lengths, *arrived, *[to_twin(rows) for rows in arrived], queries, grad_out, own_stats)
@@ -395,26 +378,27 @@
             jax.ShapeDtypeStruct(queries.shape, BF16),
             jax.ShapeDtypeStruct((chip_rows, 2 * HD), F32),
         ),
-        in_specs=[smem, hbm, vmem, vmem, vmem, vmem],
-        out_specs=(vmem, hbm),
+        in_specs=[smem, vmem, vmem, vmem, vmem, vmem],
+        out_specs=(vmem, vmem),
         scratch_shapes=[
-            pltpu.VMEM((chip_rows, 2 * HD), BF16),
-            pltpu.VMEM((chip_rows, 2 * HD), F32),
             pltpu.VMEM((2 * per_device, HD, TILE), BF16),
             turned,
             turned,
             pltpu.VMEM((HG, HD, TILE), F32),
-            pltpu.SemaphoreType.DMA((2,)),
-            pltpu.SemaphoreType.DMA((2,)),
         ],
         compiler_params=pltpu.CompilerParams(vmem_limit_bytes=32 * 2**20),
         cost_estimate=cost(20),
         name="own_grads",
     )(pair_lengths, chip, queries, grad_out, stats, dq_far)
     total = own_grad
-    for part in landed:
+    for number, part in enumerate(landed):
+        if number == SHORT:
+            part = jnp.pad(part, ((TILE, TILE), (0, 0)))
+            part = lax.dynamic_slice_in_dim(part, TILE - skipped, chip_rows, 0)
         total = total + part.astype(F32)
-    grad_kv = total[:rows_dev] + to_twin(total[rows_dev:].astype(BF16)).astype(F32)
+    own_rows = lax.dynamic_slice_in_dim(total, core * rows_dev, rows_dev, 0)
+    twin_rows = lax.dynamic_slice_in_dim(total, (1 - core) * rows_dev, rows_dev, 0)
+    grad_kv = own_rows + to_twin(twin_rows.astype(BF16)).astype(F32)
     return grad_queries, grad_kv
 
 

time: 110 us -> 107 us (0.973)
  the two profiles are of different devices: /device:TPU:9 before, /device:TPU:19 now
where the time goes in v1:
time: 107 us
  Pallas kernels  62.4 us (58%)
  starting transfers between devices  27.1 us (25%)
  waiting for transfers between devices  9.17 us (9%)
  other arithmetic  4.82 us (5%)
  local copies, waits for them, and re-layouts  2.8 us (3%)
    pallas_call x1, Pallas kernels, body(): pl.pallas_call(functools.partial(far_kernel, per_device), out_shape=(pltp...  38.5 us
    ppermute x6, starting transfers between devices, send(): return lax.ppermute(value, 'dp', pairs)  18.7 us
    pallas_call x1, Pallas kernels, body(): pl.pallas_call(functools.partial(own_grads_kernel, per_device), out_shape...  16.2 us
    ppermute x8, starting transfers between devices, to_twin(): return lax.ppermute(value, 'dp', [(i, i ^ 1) for i in range(count)])  8.44 us
    pallas_call x1, Pallas kernels, body(): pl.pallas_call(functools.partial(own_stats_kernel, per_device), out_shape...  7.57 us
    ppermute x8, waiting for transfers between devices, to_twin(): return lax.ppermute(value, 'dp', [(i, i ^ 1) for i in range(count)])  5.58 us
    convert_element_type x3, other arithmetic, body(): landed.append(send(both.astype(BF16), number, False))  3.59 us
    ppermute x6, waiting for transfers between devices, send(): return lax.ppermute(value, 'dp', pairs)  3.59 us
  transfers between devices with their start and end apart: 14, of which 5 were waited for; matrix products, arithmetic and copies ran while one was open for 4% of the time, Pallas kernels for 22%

profile of v1, /device:TPU:19, one launch (start us, length us, event | category | flops | bytes accessed | tf_op | source)
XLA Modules:
  0.0 107.1 jit_solution(5046474318881956330)
XLA Ops:
  0.6 0.0 copy-start.4
  0.6 0.0 copy-start.1
  0.7 0.0 copy-start
  0.7 0.7 collective-permute-start
  1.4 1.0 constant_dynamic-update-slice_fusion.2
  2.4 0.4 collective-permute-done
  2.8 1.0 constant_dynamic-update-slice_fusion
  3.8 3.2 %collective-permute-start.3 = (bf16[1024,256]{1,0:T(8,128)(2,1)S(1)}, bf16[1024,256]{1,0:T(8,128)(2,1)S(1)}, u32[]{:S(2)}, u32[]{:S(2)}) collective-permute-start(bf16[1024,256]{1,0:T(8,128)(2,1)S(1)} %constant_dynamic-slice_fusion.1.kv), channel_id=1, source_target_pairs={{1,5},{3,7},{4,0},{5,9},{6,2},{7,11},{8,4},{9,13},{10,6},{11,15},{... | collective-permute-start | bytes 1572872 | tf_op jit(solution)/shard_map/ppermute | solution.py:309
  7.0 3.0 %collective-permute-start.1 = (bf16[1024,256]{1,0:T(8,128)(2,1)S(1)}, bf16[1024,256]{1,0:T(8,128)(2,1)S(1)}, u32[]{:S(2)}, u32[]{:S(2)}) collective-permute-start(bf16[1024,256]{1,0:T(8,128)(2,1)S(1)} %constant_dynamic-slice_fusion.1.kv), channel_id=1, source_target_pairs={{0,2},{2,0},{3,5},{4,6},{5,3},{6,4},{7,9},{8,10},{9,7},{10,8},{11,... | collective-permute-start | bytes 1572872 | tf_op jit(solution)/shard_map/ppermute | solution.py:309
  10.1 0.1 constant_dynamic-slice_fusion
  10.2 0.0 copy-start.2
  10.2 3.2 %collective-permute-start.2 = (bf16[768,256]{1,0:T(8,128)(2,1)S(1)}, bf16[768,256]{1,0:T(8,128)(2,1)S(1)}, u32[]{:S(2)}, u32[]{:S(2)}) collective-permute-start(bf16[768,256]{1,0:T(8,128)(2,1)S(1)} %constant_dynamic-slice_fusion), channel_id=1, source_target_pairs={{0,6},{3,9},{4,10},{6,0},{7,13},{8,14},{9,3},{10,4},{13,7},{14,8},... | collective-permute-start | bytes 1179656 | tf_op jit(solution)/shard_map/ppermute | solution.py:309
  13.4 0.0 copy-done.4
  13.4 0.0 copy-done.1
  13.4 0.0 copy-done
  13.4 7.6 %own_stats.1.stats_in = f32[16,8,256]{2,1,0:T(8,128)S(1)} custom-call(s32[10]{0:T(128)S(1)} %copy-done.4, bf16[1024,256]{1,0:T(8,128)(2,1)S(1)} %constant_dynamic-slice_fusion.1.kv, bf16[512,1024]{1,0:T(8,128)(2,1)S(1)} %copy-done, bf16[512,1024]{1,0:T(8,128)(2,1)S(1)} %copy-done.1), custom_call_target="tpu_custom_call" | custom-call | flops 6442450944 | bytes 8388608 | tf_op jit(solution)/shard_map/own_stats/pallas_call | solution.py:333
  21.0 0.0 collective-permute-done.3.mine_2
  21.0 0.1 collective-permute-start.6
  21.1 3.6 %collective-permute-done.1.mine_0 = bf16[1024,256]{1,0:T(8,128)(2,1)S(1)} collective-permute-done((bf16[1024,256]{1,0:T(8,128)(2,1)S(1)}, bf16[1024,256]{1,0:T(8,128)(2,1)S(1)}, u32[]{:S(2)}, u32[]{:S(2)}) %collective-permute-start.1) | collective-permute-done | bytes 524320 | tf_op jit(solution)/shard_map/ppermute | solution.py:309
  24.6 7.0 %collective-permute-start.4 = (bf16[1024,256]{1,0:T(8,128)(2,1)S(1)}, bf16[1024,256]{1,0:T(8,128)(2,1)S(1)}, u32[]{:S(2)}, u32[]{:S(2)}) collective-permute-start(bf16[1024,256]{1,0:T(8,128)(2,1)S(1)} %collective-permute-done.1.mine_0), channel_id=1, source_target_pairs={{0,1},{1,0},{2,3},{3,2},{4,5},{5,4},{6,7},{7,6},{8,9},{9,8},{10,11... | collective-permute-start | bytes 1572872 | tf_op jit(solution)/shard_map/ppermute | solution.py:312
  31.7 0.0 collective-permute-done.2.mine_1
  31.7 0.0 collective-permute-start.5
  31.7 2.1 %collective-permute-done.5.twin_1 = bf16[768,256]{1,0:T(8,128)(2,1)S(1)} collective-permute-done((bf16[768,256]{1,0:T(8,128)(2,1)S(1)}, bf16[768,256]{1,0:T(8,128)(2,1)S(1)}, u32[]{:S(2)}, u32[]{:S(2)}) %collective-permute-start.5) | collective-permute-done | bytes 393248 | tf_op jit(solution)/shard_map/ppermute | solution.py:312
  33.8 0.0 collective-permute-done.6.twin_2
  33.8 0.0 collective-permute-done.4.twin_0
  33.8 0.0 copy-done.2
  33.8 38.5 %far.1 = (f32[16,128,256]{2,1,0:T(8,128)}, f32[16,8,256]{2,1,0:T(8,128)S(1)}, bf16[1024,256]{1,0:T(8,128)(2,1)S(1)}, bf16[768,256]{1,0:T(8,128)(2,1)S(1)}, bf16[...) custom-call(s32[10]{0:T(128)S(1)} %copy-done.4, ...), custom_call_target="tpu_custom_call" | custom-call | flops 32212254720 | bytes 8388608 | tf_op jit(solution)/shard_map/far/pallas_call | solution.py:346
  72.4 0.6 copy-done.6
  73.0 0.0 collective-permute-start.9
  73.0 0.5 collective-permute-start.7
  73.5 0.0 collective-permute-start.11
  73.5 1.6 %collective-permute-done.9 = bf16[768,256]{1,0:T(8,128)(2,1)} collective-permute-done((bf16[768,256]{1,0:T(8,128)(2,1)}, bf16[768,256]{1,0:T(8,128)(2,1)}, u32[]{:S(2)}, u32[]{:S(2)}) %collective-permute-start.9) | collective-permute-done | bytes 393248 | tf_op jit(solution)/shard_map/ppermute | solution.py:312
  75.1 1.2 %add_convert_fusion.2 = bf16[768,256]{1,0:T(8,128)(2,1)S(1)} fusion(bf16[768,256]{1,0:T(8,128)(2,1)} %collective-permute-done.9, bf16[768,256]{1,0:T(8,128)(2,1)S(1)} %get-tuple-element.24), kind=kLoop, calls=%fused_computation.3 | loop fusion | flops 786432 | bytes 1179648 | tf_op jit(solution)/shard_map/convert_element_type | solution.py:374
  76.3 1.9 %collective-permute-start.10 = (bf16[768,256]{1,0:T(8,128)(2,1)S(1)}, bf16[768,256]{1,0:T(8,128)(2,1)S(1)}, u32[]{:S(2)}, u32[]{:S(2)}) collective-permute-start(bf16[768,256]{1,0:T(8,128)(2,1)S(1)} %add_convert_fusion.2), channel_id=1, source_target_pairs={{0,6},{3,9},{4,10},{6,0},{7,13},{8,14},{9,3},{10,4},{13,7},{14,8},... | collective-permute-start | bytes 1179656 | tf_op jit(solution)/shard_map/ppermute | solution.py:309
  78.2 0.0 collective-permute-done.7
  78.2 1.2 %add_convert_fusion.1 = bf16[1024,256]{1,0:T(8,128)(2,1)S(1)} fusion(bf16[1024,256]{1,0:T(8,128)(2,1)} %collective-permute-done.7, bf16[1024,256]{1,0:T(8,128)(2,1)S(1)} %get-tuple-element.22), kind=kLoop, calls=%fused_computation.2 | loop fusion | flops 1048576 | bytes 1572864 | tf_op jit(solution)/shard_map/convert_element_type | solution.py:374
  79.4 1.9 %collective-permute-start.8 = (bf16[1024,256]{1,0:T(8,128)(2,1)S(1)}, bf16[1024,256]{1,0:T(8,128)(2,1)S(1)}, u32[]{:S(2)}, u32[]{:S(2)}) collective-permute-start(bf16[1024,256]{1,0:T(8,128)(2,1)S(1)} %add_convert_fusion.1), channel_id=1, source_target_pairs={{0,2},{2,0},{3,5},{4,6},{5,3},{6,4},{7,9},{8,10},{9,7},{10,8},{11,... | collective-permute-start | bytes 1572872 | tf_op jit(solution)/shard_map/ppermute | solution.py:309
  81.3 0.0 collective-permute-done.11
  81.4 1.2 %add_convert_fusion = bf16[1024,256]{1,0:T(8,128)(2,1)S(1)} fusion(bf16[1024,256]{1,0:T(8,128)(2,1)} %collective-permute-done.11, bf16[1024,256]{1,0:T(8,128)(2,1)S(1)} %get-tuple-element.26), kind=kLoop, calls=%fused_computation.1 | loop fusion | flops 1048576 | bytes 1572864 | tf_op jit(solution)/shard_map/convert_element_type | solution.py:374
  82.5 5.4 %collective-permute-start.12 = (bf16[1024,256]{1,0:T(8,128)(2,1)S(1)}, bf16[1024,256]{1,0:T(8,128)(2,1)S(1)}, u32[]{:S(2)}, u32[]{:S(2)}) collective-permute-start(bf16[1024,256]{1,0:T(8,128)(2,1)S(1)} %add_convert_fusion), channel_id=1, source_target_pairs={{0,4},{2,6},{4,8},{5,1},{6,10},{7,3},{8,12},{9,5},{10,14},{11,7},{... | collective-permute-start | bytes 1572872 | tf_op jit(solution)/shard_map/ppermute | solution.py:309
  88.0 16.2 %own_grads.1 = (bf16[512,1024]{1,0:T(8,128)(2,1)}, f32[1024,256]{1,0:T(8,128)S(1)}) custom-call(s32[10]{0:T(128)S(1)} %copy-done.4, bf16[1024,256]{1,0:T(8,128)(2,1)S(1)} %constant_dynamic-slice_fusion.1.kv, bf16[512,1024]{1,0:T(8,128)(2,1)S(1)} %copy-done, bf16[512,1024]{1,0:T(8,128)(2,1)S(1)} %copy-done.3, f32[16,8,256]{2,1,0:T(8,128)S(1)} %copy-done.7, ...), custom_call_target="tpu_custom_call" | custom-call | flops 16106127360 | bytes 8388608 | tf_op jit(solution)/shard_map/own_grads/pallas_call | solution.py:375
  104.2 0.0 collective-permute-done.10
  104.2 0.0 collective-permute-done.8
  104.2 0.0 collective-permute-done.12
  104.3 0.4 convert_add_fusion
  104.7 0.1 collective-permute-start.13
  104.8 1.5 %collective-permute-done.13 = bf16[512,256]{1,0:T(8,128)(2,1)S(1)} collective-permute-done((bf16[512,256]{1,0:T(8,128)(2,1)S(1)}, bf16[512,256]{1,0:T(8,128)(2,1)S(1)}, u32[]{:S(2)}, u32[]{:S(2)}) %collective-permute-start.13) | collective-permute-done | bytes 262176 | tf_op jit(solution)/shard_map/ppermute | solution.py:312
  106.3 0.8 convert_add_fusion.1
  (10 shorter events, 0.1 us)
Async XLA Ops:
  0.6 12.7 %copy-start.4 = (s32[10]{0:T(128)S(1)}, s32[10]{0:T(128)}, u32[]{:S(2)}) copy-start(s32[10]{0:T(128)} %lengths.5) | copy-start | bytes 124
  0.6 12.7 %copy-start.1 = (bf16[512,1024]{1,0:T(8,128)(2,1)S(1)}, bf16[512,1024]{1,0:T(8,128)(2,1)}, u32[]{:S(2)}) copy-start(bf16[512,1024]{1,0:T(8,128)(2,1)} %g_ref.5) | copy-start | bytes 3145732
  0.7 12.7 %copy-start = (bf16[512,1024]{1,0:T(8,128)(2,1)S(1)}, bf16[512,1024]{1,0:T(8,128)(2,1)}, u32[]{:S(2)}) copy-start(bf16[512,1024]{1,0:T(8,128)(2,1)} %q_ref.5) | copy-start | bytes 3145732
  0.7 2.1 %collective-permute-start = (bf16[512,256]{1,0:T(8,128)(2,1)}, bf16[512,256]{1,0:T(8,128)(2,1)S(1)}, u32[]{:S(2)}, u32[]{:S(2)}) collective-permute-start(bf16[512,256]{1,0:T(8,128)(2,1)} %param.5), channel_id=1, source_target_pairs={{0,1},{1,0},{2,3},{3,2},{4,5},{5,4},{6,7},{7,6},{8,9},{9,8},{10,11... | collective-permute-start | bytes 786440 | tf_op jit(solution)/shard_map/ppermute | solution.py:312
  3.8 17.2 %collective-permute-start.3 = (bf16[1024,256]{1,0:T(8,128)(2,1)S(1)}, bf16[1024,256]{1,0:T(8,128)(2,1)S(1)}, u32[]{:S(2)}, u32[]{:S(2)}) collective-permute-start(bf16[1024,256]{1,0:T(8,128)(2,1)S(1)} %constant_dynamic-slice_fusion.1.kv), channel_id=1, source_target_pairs={{1,5},{3,7},{4,0},{5,9},{6,2},{7,11},{8,4},{9,13},{10,6},{11,15},{... | collective-permute-start | bytes 1572872 | tf_op jit(solution)/shard_map/ppermute | solution.py:309
  7.0 17.6 %collective-permute-start.1 = (bf16[1024,256]{1,0:T(8,128)(2,1)S(1)}, bf16[1024,256]{1,0:T(8,128)(2,1)S(1)}, u32[]{:S(2)}, u32[]{:S(2)}) collective-permute-start(bf16[1024,256]{1,0:T(8,128)(2,1)S(1)} %constant_dynamic-slice_fusion.1.kv), channel_id=1, source_target_pairs={{0,2},{2,0},{3,5},{4,6},{5,3},{6,4},{7,9},{8,10},{9,7},{10,8},{11,... | collective-permute-start | bytes 1572872 | tf_op jit(solution)/shard_map/ppermute | solution.py:309
  10.2 23.6 %copy-start.2 = (bf16[512,1024]{1,0:T(8,128)(2,1)S(1)}, bf16[512,1024]{1,0:T(8,128)(2,1)}, u32[]{:S(2)}) copy-start(bf16[512,1024]{1,0:T(8,128)(2,1)} %g_ref.5) | copy-start | bytes 3145732
  10.2 21.5 %collective-permute-start.2 = (bf16[768,256]{1,0:T(8,128)(2,1)S(1)}, bf16[768,256]{1,0:T(8,128)(2,1)S(1)}, u32[]{:S(2)}, u32[]{:S(2)}) collective-permute-start(bf16[768,256]{1,0:T(8,128)(2,1)S(1)} %constant_dynamic-slice_fusion), channel_id=1, source_target_pairs={{0,6},{3,9},{4,10},{6,0},{7,13},{8,14},{9,3},{10,4},{13,7},{14,8},... | collective-permute-start | bytes 1179656 | tf_op jit(solution)/shard_map/ppermute | solution.py:309
  21.0 12.8 %collective-permute-start.6 = (bf16[1024,256]{1,0:T(8,128)(2,1)S(1)}, bf16[1024,256]{1,0:T(8,128)(2,1)S(1)}, u32[]{:S(2)}, u32[]{:S(2)}) collective-permute-start(bf16[1024,256]{1,0:T(8,128)(2,1)S(1)} %collective-permute-done.3.mine_2), channel_id=1, source_target_pairs={{0,1},{1,0},{2,3},{3,2},{4,5},{5,4},{6,7},{7,6},{8,9},{9,8},{10,11... | collective-permute-start | bytes 1572872 | tf_op jit(solution)/shard_map/ppermute | solution.py:312
  24.6 9.1 %collective-permute-start.4 = (bf16[1024,256]{1,0:T(8,128)(2,1)S(1)}, bf16[1024,256]{1,0:T(8,128)(2,1)S(1)}, u32[]{:S(2)}, u32[]{:S(2)}) collective-permute-start(bf16[1024,256]{1,0:T(8,128)(2,1)S(1)} %collective-permute-done.1.mine_0), channel_id=1, source_target_pairs={{0,1},{1,0},{2,3},{3,2},{4,5},{5,4},{6,7},{7,6},{8,9},{9,8},{10,11... | collective-permute-start | bytes 1572872 | tf_op jit(solution)/shard_map/ppermute | solution.py:312
  31.7 2.1 %collective-permute-start.5 = (bf16[768,256]{1,0:T(8,128)(2,1)S(1)}, bf16[768,256]{1,0:T(8,128)(2,1)S(1)}, u32[]{:S(2)}, u32[]{:S(2)}) collective-permute-start(bf16[768,256]{1,0:T(8,128)(2,1)S(1)} %collective-permute-done.2.mine_1), channel_id=1, source_target_pairs={{0,1},{1,0},{2,3},{3,2},{4,5},{5,4},{6,7},{7,6},{8,9},{9,8},{10,11... | collective-permute-start | bytes 1179656 | tf_op jit(solution)/shard_map/ppermute | solution.py:312
  72.3 0.6 copy-start.6
  73.0 2.1 %collective-permute-start.9 = (bf16[768,256]{1,0:T(8,128)(2,1)}, bf16[768,256]{1,0:T(8,128)(2,1)}, u32[]{:S(2)}, u32[]{:S(2)}) collective-permute-start(bf16[768,256]{1,0:T(8,128)(2,1)} %get-tuple-element.25), channel_id=1, source_target_pairs={{0,1},{1,0},{2,3},{3,2},{4,5},{5,4},{6,7},{7,6},{8,9},{9,8},{10,11... | collective-permute-start | bytes 1179656 | tf_op jit(solution)/shard_map/ppermute | solution.py:312
  73.0 5.2 %collective-permute-start.7 = (bf16[1024,256]{1,0:T(8,128)(2,1)}, bf16[1024,256]{1,0:T(8,128)(2,1)}, u32[]{:S(2)}, u32[]{:S(2)}) collective-permute-start(bf16[1024,256]{1,0:T(8,128)(2,1)} %get-tuple-element.23), channel_id=1, source_target_pairs={{0,1},{1,0},{2,3},{3,2},{4,5},{5,4},{6,7},{7,6},{8,9},{9,8},{10,11... | collective-permute-start | bytes 1572872 | tf_op jit(solution)/shard_map/ppermute | solution.py:312
  73.5 7.9 %collective-permute-start.11 = (bf16[1024,256]{1,0:T(8,128)(2,1)S(1)}, bf16[1024,256]{1,0:T(8,128)(2,1)}, u32[]{:S(2)}, u32[]{:S(2)}) collective-permute-start(bf16[1024,256]{1,0:T(8,128)(2,1)S(1)} %get-tuple-element.27), channel_id=1, source_target_pairs={{0,1},{1,0},{2,3},{3,2},{4,5},{5,4},{6,7},{7,6},{8,9},{9,8},{10,11... | collective-permute-start | bytes 1572872 | tf_op jit(solution)/shard_map/ppermute | solution.py:312
  75.0 12.9 %copy-start.3 = (bf16[512,1024]{1,0:T(8,128)(2,1)S(1)}, bf16[512,1024]{1,0:T(8,128)(2,1)}, u32[]{:S(2)}) copy-start(bf16[512,1024]{1,0:T(8,128)(2,1)} %g_ref.5) | copy-start | bytes 3145732
  75.1 12.9 %copy-start.5 = (f32[16,128,256]{2,1,0:T(8,128)S(1)}, f32[16,128,256]{2,1,0:T(8,128)}, u32[]{:S(2)}) copy-start(f32[16,128,256]{2,1,0:T(8,128)} %get-tuple-element.19.dq_in) | copy-start | bytes 6291460
  75.1 12.9 %copy-start.7 = (f32[16,8,256]{2,1,0:T(8,128)S(1)}, f32[16,8,256]{2,1,0:T(8,128)}, u32[]{:S(2)}) copy-start(f32[16,8,256]{2,1,0:T(8,128)} %copy-done.6) | copy-start | bytes 393220
  76.3 27.9 %collective-permute-start.10 = (bf16[768,256]{1,0:T(8,128)(2,1)S(1)}, bf16[768,256]{1,0:T(8,128)(2,1)S(1)}, u32[]{:S(2)}, u32[]{:S(2)}) collective-permute-start(bf16[768,256]{1,0:T(8,128)(2,1)S(1)} %add_convert_fusion.2), channel_id=1, source_target_pairs={{0,6},{3,9},{4,10},{6,0},{7,13},{8,14},{9,3},{10,4},{13,7},{14,8},... | collective-permute-start | bytes 1179656 | tf_op jit(solution)/shard_map/ppermute | solution.py:309
  79.4 24.8 %collective-permute-start.8 = (bf16[1024,256]{1,0:T(8,128)(2,1)S(1)}, bf16[1024,256]{1,0:T(8,128)(2,1)S(1)}, u32[]{:S(2)}, u32[]{:S(2)}) collective-permute-start(bf16[1024,256]{1,0:T(8,128)(2,1)S(1)} %add_convert_fusion.1), channel_id=1, source_target_pairs={{0,2},{2,0},{3,5},{4,6},{5,3},{6,4},{7,9},{8,10},{9,7},{10,8},{11,... | collective-permute-start | bytes 1572872 | tf_op jit(solution)/shard_map/ppermute | solution.py:309
  82.5 21.7 %collective-permute-start.12 = (bf16[1024,256]{1,0:T(8,128)(2,1)S(1)}, bf16[1024,256]{1,0:T(8,128)(2,1)S(1)}, u32[]{:S(2)}, u32[]{:S(2)}) collective-permute-start(bf16[1024,256]{1,0:T(8,128)(2,1)S(1)} %add_convert_fusion), channel_id=1, source_target_pairs={{0,4},{2,6},{4,8},{5,1},{6,10},{7,3},{8,12},{9,5},{10,14},{11,7},{... | collective-permute-start | bytes 1572872 | tf_op jit(solution)/shard_map/ppermute | solution.py:309
  104.7 1.6 %collective-permute-start.13 = (bf16[512,256]{1,0:T(8,128)(2,1)S(1)}, bf16[512,256]{1,0:T(8,128)(2,1)S(1)}, u32[]{:S(2)}, u32[]{:S(2)}) collective-permute-start(bf16[512,256]{1,0:T(8,128)(2,1)S(1)} %dynamic-slice_convert_fusion), channel_id=1, source_target_pairs={{0,1},{1,0},{2,3},{3,2},{4,5},{5,4},{6,7},{7,6},{8,9},{9,8},{10,11... | collective-permute-start | bytes 786440 | tf_op jit(solution)/shard_map/ppermute | solution.py:312

commit v2 on v1

--- a/solution.py
+++ b/solution.py
@@ -246,14 +246,21 @@
 
 
 def own_grads_kernel(
-    per_device, lengths, kv, q_ref, g_ref, stats_ref, dq_in, dq_ref, acc, keys_t, q_t, g_t, dq_t
+    per_device, tile, lengths, kv, q_ref, g_ref, stats_ref, dq_in, *rest
 ):
-    acc[...] = jnp.zeros_like(acc)
+    if tile == 0:
+        dq_ref, acc, keys_t, q_t, g_t, dq_t = rest
+        acc[...] = jnp.zeros_like(acc)
+    else:
+        acc_in, _, dq_ref, acc, keys_t, q_t, g_t, dq_t = rest
+        acc[...] = acc_in[...]
     for block in range(2 * per_device):
         keys_t[block] = kv[block * TILE : (block + 1) * TILE, :HD].T
 
     def unit(index, _):
-        place = Place(lengths, per_device, index)
+        place = Place(lengths, per_device, tile * GROUPS + index)
+        place.rows = pl.ds(0, TILE)
+        place.slot = index * HG
         turn_rows(place, q_ref, g_ref, q_t, g_t)
         for head in range(HG):
             dq_t[head] = dq_in[place.slot + head]
@@ -284,7 +291,7 @@
             dq_ref[place.rows, place.cols(head)] = (dq_t[head] * SCALE).T.astype(BF16)
         return 0
 
-    lax.fori_loop(0, per_device * GROUPS, unit, 0)
+    lax.fori_loop(0, GROUPS, unit, 0)
 
 
 def body(queries, kv_cache, grad_out, pair_lengths):
@@ -368,28 +375,51 @@
         name="far",
     )(pair_lengths, *arrived, *[to_twin(rows) for rows in arrived], queries, grad_out, own_stats)
 
-    landed = []
+    leaving = []
     for number in range(len(ROUNDS)):
         both = partial[number].astype(F32) + to_twin(partial[len(ROUNDS) + number]).astype(F32)
-        landed.append(send(both.astype(BF16), number, False))
-    grad_queries, own_grad = pl.pallas_call(
-        functools.partial(own_grads_kernel, per_device),
-        out_shape=(
-            jax.ShapeDtypeStruct(queries.shape, BF16),
-            jax.ShapeDtypeStruct((chip_rows, 2 * HD), F32),
-        ),
-        in_specs=[smem, vmem, vmem, vmem, vmem, vmem],
-        out_specs=(vmem, vmem),
-        scratch_shapes=[
-            pltpu.VMEM((2 * per_device, HD, TILE), BF16),
-            turned,
-            turned,
-            pltpu.VMEM((HG, HD, TILE), F32),
-        ],
-        compiler_params=pltpu.CompilerParams(vmem_limit_bytes=32 * 2**20),
-        cost_estimate=cost(20),
-        name="own_grads",
-    )(pair_lengths, chip, queries, grad_out, stats, dq_far)
+        leaving.append(both.astype(BF16))
+
+    def own_grads(tile, stats, before):
+        def rows_of(*block):
+            return pl.BlockSpec(block, lambda i: (tile,) + (0,) * (len(block) - 1))
+
+        return pl.pallas_call(
+            functools.partial(own_grads_kernel, per_device, tile),
+            out_shape=(
+                jax.ShapeDtypeStruct(queries.shape, BF16),
+                jax.ShapeDtypeStruct((chip_rows, 2 * HD), F32),
+            ),
+            grid=(1,),
+            in_specs=[
+                smem,
+                vmem,
+                rows_of(TILE, QH * HD),
+                rows_of(TILE, QH * HD),
+                rows_of(QH, 8, TILE),
+                rows_of(QH, HD, TILE),
+            ]
+            + ([vmem, hbm] if before else []),
+            out_specs=(rows_of(TILE, QH * HD), vmem),
+            scratch_shapes=[
+                pltpu.VMEM((2 * per_device, HD, TILE), BF16),
+                turned,
+                turned,
+                pltpu.VMEM((HG, HD, TILE), F32),
+            ],
+            input_output_aliases={7: 0} if before else {},
+            compiler_params=pltpu.CompilerParams(vmem_limit_bytes=32 * 2**20),
+            cost_estimate=cost(10),
+            name="own_grads",
+        )(pair_lengths, chip, queries, grad_out, stats, dq_far, *before)
+
+    stats, *leaving = lax.optimization_barrier((stats, *leaving))
+    landed = [send(leaving[number], number, False) for number in range(len(ROUNDS) - 1)]
+    grad_queries, own_grad = own_grads(0, stats, ())
+    last, own_grad = lax.optimization_barrier((leaving[-1], own_grad))
+    landed.append(send(last, len(ROUNDS) - 1, False))
+    for tile in range(1, per_device):
+        grad_queries, own_grad = own_grads(tile, stats, (own_grad, grad_queries))
     total = own_grad
     for number, part in enumerate(landed):
         if number == SHORT:

time: 107 us -> 110 us (1.028)
  the two profiles are of different devices: /device:TPU:19 before, /device:TPU:0 now
where the time goes in v2:
time: 110 us
  starting transfers between devices  65.5 us (60%)
  Pallas kernels  29.7 us (27%)
  waiting for transfers between devices  5.97 us (5%)
  other arithmetic  4.82 us (4%)
  local copies, waits for them, and re-layouts  2.91 us (3%)
    ppermute x6, starting transfers between devices, send(): return lax.ppermute(value, 'dp', pairs)  42.5 us
    ppermute x8, starting transfers between devices, to_twin(): return lax.ppermute(value, 'dp', [(i, i ^ 1) for i in range(count)])  23 us
    pallas_call x2, Pallas kernels, own_grads(): pl.pallas_call(functools.partial(own_grads_kernel, per_device, tile), out...  17.8 us
    pallas_call x1, Pallas kernels, body(): pl.pallas_call(functools.partial(own_stats_kernel, per_device), out_shape...  7.57 us
    ppermute x8, waiting for transfers between devices, to_twin(): return lax.ppermute(value, 'dp', [(i, i ^ 1) for i in range(count)])  5.68 us
    pallas_call x1, Pallas kernels, body(): pl.pallas_call(functools.partial(far_kernel, per_device), out_shape=(pltp...  4.36 us
    convert_element_type x3, other arithmetic, body(): leaving.append(both.astype(BF16))  3.59 us
  transfers between devices with their start and end apart: 14, of which 6 were waited for; matrix products, arithmetic and copies ran while one was open for 3% of the time, Pallas kernels for 23%

profile of v2, /device:TPU:0, one launch (start us, length us, event | category | flops | bytes accessed | tf_op | source)
XLA Modules:
  0.0 109.8 jit_solution(17678219686843010906)
XLA Ops:
  0.6 0.0 copy-start.4
  0.6 0.0 copy-start.1
  0.7 0.0 copy-start
  0.7 0.5 collective-permute-start
  1.2 1.1 constant_dynamic-update-slice_fusion.2
  2.2 0.3 collective-permute-done
  2.6 1.0 constant_dynamic-update-slice_fusion
  3.6 1.3 %collective-permute-start.3 = (bf16[1024,256]{1,0:T(8,128)(2,1)S(1)}, bf16[1024,256]{1,0:T(8,128)(2,1)S(1)}, u32[]{:S(2)}, u32[]{:S(2)}) collective-permute-start(bf16[1024,256]{1,0:T(8,128)(2,1)S(1)} %constant_dynamic-slice_fusion.1.kv), channel_id=1, source_target_pairs={{1,5},{3,7},{4,0},{5,9},{6,2},{7,11},{8,4},{9,13},{10,6},{11,15},{... | collective-permute-start | bytes 1572872 | tf_op jit(solution)/shard_map/ppermute | solution.py:316
  4.9 4.8 %collective-permute-start.1 = (bf16[1024,256]{1,0:T(8,128)(2,1)S(1)}, bf16[1024,256]{1,0:T(8,128)(2,1)S(1)}, u32[]{:S(2)}, u32[]{:S(2)}) collective-permute-start(bf16[1024,256]{1,0:T(8,128)(2,1)S(1)} %constant_dynamic-slice_fusion.1.kv), channel_id=1, source_target_pairs={{0,2},{2,0},{3,5},{4,6},{5,3},{6,4},{7,9},{8,10},{9,7},{10,8},{11,... | collective-permute-start | bytes 1572872 | tf_op jit(solution)/shard_map/ppermute | solution.py:316
  9.7 0.1 constant_dynamic-slice_fusion
  9.8 0.0 copy-start.2
  9.8 4.2 %collective-permute-start.2 = (bf16[768,256]{1,0:T(8,128)(2,1)S(1)}, bf16[768,256]{1,0:T(8,128)(2,1)S(1)}, u32[]{:S(2)}, u32[]{:S(2)}) collective-permute-start(bf16[768,256]{1,0:T(8,128)(2,1)S(1)} %constant_dynamic-slice_fusion), channel_id=1, source_target_pairs={{0,6},{3,9},{4,10},{6,0},{7,13},{8,14},{9,3},{10,4},{13,7},{14,8},... | collective-permute-start | bytes 1179656 | tf_op jit(solution)/shard_map/ppermute | solution.py:316
  14.0 0.0 copy-done.4
  14.0 0.0 copy-done.1
  14.0 0.0 copy-done
  14.1 7.6 %own_stats.1.stats_in = f32[16,8,256]{2,1,0:T(8,128)S(1)} custom-call(s32[10]{0:T(128)S(1)} %copy-done.4, bf16[1024,256]{1,0:T(8,128)(2,1)S(1)} %constant_dynamic-slice_fusion.1.kv, bf16[512,1024]{1,0:T(8,128)(2,1)S(1)} %copy-done, bf16[512,1024]{1,0:T(8,128)(2,1)S(1)} %copy-done.1), custom_call_target="tpu_custom_call" | custom-call | flops 6442450944 | bytes 8388608 | tf_op jit(solution)/shard_map/own_stats/pallas_call | solution.py:340
  21.6 0.0 collective-permute-done.3.mine_2
  21.6 0.1 collective-permute-start.6
  21.7 0.3 collective-permute-done.1.mine_0
  22.0 0.2 collective-permute-start.4
  22.2 0.0 collective-permute-done.2.mine_1
  22.2 0.3 collective-permute-start.5
  22.5 2.4 %collective-permute-done.5.twin_1 = bf16[768,256]{1,0:T(8,128)(2,1)S(1)} collective-permute-done((bf16[768,256]{1,0:T(8,128)(2,1)S(1)}, bf16[768,256]{1,0:T(8,128)(2,1)S(1)}, u32[]{:S(2)}, u32[]{:S(2)}) %collective-permute-start.5) | collective-permute-done | bytes 393248 | tf_op jit(solution)/shard_map/ppermute | solution.py:319
  24.9 0.0 collective-permute-done.6.twin_2
  24.9 0.0 collective-permute-done.4.twin_0
  24.9 4.4 %far.1 = (f32[16,128,256]{2,1,0:T(8,128)}, f32[16,8,256]{2,1,0:T(8,128)S(1)}, bf16[1024,256]{1,0:T(8,128)(2,1)S(1)}, bf16[768,256]{1,0:T(8,128)(2,1)S(1)}, bf16[...) custom-call(s32[10]{0:T(128)S(1)} %copy-done.4, ...), custom_call_target="tpu_custom_call" | custom-call | flops 32212254720 | bytes 8388608 | tf_op jit(solution)/shard_map/far/pallas_call | solution.py:353
  29.3 0.6 copy-done.6
  30.0 21.3 %collective-permute-start.8 = (bf16[768,256]{1,0:T(8,128)(2,1)}, bf16[768,256]{1,0:T(8,128)(2,1)}, u32[]{:S(2)}, u32[]{:S(2)}) collective-permute-start(bf16[768,256]{1,0:T(8,128)(2,1)} %get-tuple-element.30), channel_id=1, source_target_pairs={{0,1},{1,0},{2,3},{3,2},{4,5},{5,4},{6,7},{7,6},{8,9},{9,8},{10,11... | collective-permute-start | bytes 1179656 | tf_op jit(solution)/shard_map/ppermute | solution.py:319
  51.3 0.0 collective-permute-start.7
  51.3 0.5 collective-permute-start.9
  51.8 1.2 %collective-permute-done.8 = bf16[768,256]{1,0:T(8,128)(2,1)} collective-permute-done((bf16[768,256]{1,0:T(8,128)(2,1)}, bf16[768,256]{1,0:T(8,128)(2,1)}, u32[]{:S(2)}, u32[]{:S(2)}) %collective-permute-start.8) | collective-permute-done | bytes 393248 | tf_op jit(solution)/shard_map/ppermute | solution.py:319
  53.0 1.2 %add_convert_fusion.2 = bf16[768,256]{1,0:T(8,128)(2,1)S(1)} fusion(bf16[768,256]{1,0:T(8,128)(2,1)} %collective-permute-done.8, bf16[768,256]{1,0:T(8,128)(2,1)S(1)} %get-tuple-element.29), kind=kLoop, calls=%fused_computation.3 | loop fusion | flops 786432 | bytes 1179648 | tf_op jit(solution)/shard_map/convert_element_type | solution.py:381
  54.2 0.2 collective-permute-done.7
  54.4 1.2 %add_convert_fusion.1 = bf16[1024,256]{1,0:T(8,128)(2,1)S(1)} fusion(bf16[1024,256]{1,0:T(8,128)(2,1)} %collective-permute-done.7, bf16[1024,256]{1,0:T(8,128)(2,1)S(1)} %get-tuple-element.27), kind=kLoop, calls=%fused_computation.2 | loop fusion | flops 1048576 | bytes 1572864 | tf_op jit(solution)/shard_map/convert_element_type | solution.py:381
  55.6 0.0 collective-permute-done.9
  55.6 1.2 %add_convert_fusion = bf16[1024,256]{1,0:T(8,128)(2,1)S(1)} fusion(bf16[1024,256]{1,0:T(8,128)(2,1)} %collective-permute-done.9, bf16[1024,256]{1,0:T(8,128)(2,1)S(1)} %get-tuple-element.31), kind=kLoop, calls=%fused_computation.1 | loop fusion | flops 1048576 | bytes 1572864 | tf_op jit(solution)/shard_map/convert_element_type | solution.py:381
  56.8 27.7 %collective-permute-start.11 = (bf16[768,256]{1,0:T(8,128)(2,1)S(1)}, bf16[768,256]{1,0:T(8,128)(2,1)S(1)}, u32[]{:S(2)}, u32[]{:S(2)}) collective-permute-start(bf16[768,256]{1,0:T(8,128)(2,1)S(1)} %add_convert_fusion.2), channel_id=1, source_target_pairs={{0,6},{3,9},{4,10},{6,0},{7,13},{8,14},{9,3},{10,4},{13,7},{14,8},... | collective-permute-start | bytes 1179656 | tf_op jit(solution)/shard_map/ppermute | solution.py:316
  84.5 1.9 %collective-permute-start.10 = (bf16[1024,256]{1,0:T(8,128)(2,1)S(1)}, bf16[1024,256]{1,0:T(8,128)(2,1)S(1)}, u32[]{:S(2)}, u32[]{:S(2)}) collective-permute-start(bf16[1024,256]{1,0:T(8,128)(2,1)S(1)} %add_convert_fusion.1), channel_id=1, source_target_pairs={{0,2},{2,0},{3,5},{4,6},{5,3},{6,4},{7,9},{8,10},{9,7},{10,8},{11,... | collective-permute-start | bytes 1572872 | tf_op jit(solution)/shard_map/ppermute | solution.py:316
  86.5 8.9 %own_grads.2 = (bf16[512,1024]{1,0:T(8,128)(2,1)}, f32[1024,256]{1,0:T(8,128)S(1)}) custom-call(s32[10]{0:T(128)S(1)} %copy-done.4, bf16[1024,256]{1,0:T(8,128)(2,1)S(1)} %constant_dynamic-slice_fusion.1.kv, bf16[512,1024]{1,0:T(8,128)(2,1)S(1)} %copy-done, bf16[512,1024]{1,0:T(8,128)(2,1)S(1)} %copy-done.3, f32[16,8,256]{2,1,0:T(8,128)S(1)} %copy-done.7, ...), custom_call_target="tpu_custom_call" | custom-call | flops 8053063680 | bytes 8388608 | tf_op jit(solution)/shard_map/own_grads/pallas_call | solution.py:387
  95.3 2.6 %collective-permute-start.12 = (bf16[1024,256]{1,0:T(8,128)(2,1)S(1)}, bf16[1024,256]{1,0:T(8,128)(2,1)S(1)}, u32[]{:S(2)}, u32[]{:S(2)}) collective-permute-start(bf16[1024,256]{1,0:T(8,128)(2,1)S(1)} %add_convert_fusion), channel_id=1, source_target_pairs={{0,4},{2,6},{4,8},{5,1},{6,10},{7,3},{8,12},{9,5},{10,14},{11,7},{... | collective-permute-start | bytes 1572872 | tf_op jit(solution)/shard_map/ppermute | solution.py:316
  98.0 8.9 %own_grads.3 = (bf16[512,1024]{1,0:T(8,128)(2,1)}, f32[1024,256]{1,0:T(8,128)S(1)}) custom-call(s32[10]{0:T(128)S(1)} %copy-done.4, bf16[1024,256]{1,0:T(8,128)(2,1)S(1)} %constant_dynamic-slice_fusion.1.kv, bf16[512,1024]{1,0:T(8,128)(2,1)S(1)} %copy-done, bf16[512,1024]{1,0:T(8,128)(2,1)S(1)} %copy-done.3, ...), custom_call_target="tpu_custom_call", output_to_operand_aliasing={{0}: (7, {})} | custom-call | flops 8053063680 | bytes 8388608 | tf_op jit(solution)/shard_map/own_grads/pallas_call | solution.py:387
  106.9 0.0 collective-permute-done.11
  106.9 0.0 collective-permute-done.10
  106.9 0.0 collective-permute-done.12
  106.9 0.4 convert_add_fusion
  107.3 0.1 collective-permute-start.13
  107.4 1.5 %collective-permute-done.13 = bf16[512,256]{1,0:T(8,128)(2,1)S(1)} collective-permute-done((bf16[512,256]{1,0:T(8,128)(2,1)S(1)}, bf16[512,256]{1,0:T(8,128)(2,1)S(1)}, u32[]{:S(2)}, u32[]{:S(2)}) %collective-permute-start.13) | collective-permute-done | bytes 262176 | tf_op jit(solution)/shard_map/ppermute | solution.py:319
  108.9 0.8 convert_add_fusion.1
  (11 shorter events, 0.1 us)
Async XLA Ops:
  0.6 13.4 %copy-start.4 = (s32[10]{0:T(128)S(1)}, s32[10]{0:T(128)}, u32[]{:S(2)}) copy-start(s32[10]{0:T(128)} %lengths.7) | copy-start | bytes 124
  0.6 13.4 %copy-start.1 = (bf16[512,1024]{1,0:T(8,128)(2,1)S(1)}, bf16[512,1024]{1,0:T(8,128)(2,1)}, u32[]{:S(2)}) copy-start(bf16[512,1024]{1,0:T(8,128)(2,1)} %g_ref.7) | copy-start | bytes 3145732
  0.7 13.4 %copy-start = (bf16[512,1024]{1,0:T(8,128)(2,1)S(1)}, bf16[512,1024]{1,0:T(8,128)(2,1)}, u32[]{:S(2)}) copy-start(bf16[512,1024]{1,0:T(8,128)(2,1)} %q_ref.7) | copy-start | bytes 3145732
  0.7 1.9 %collective-permute-start = (bf16[512,256]{1,0:T(8,128)(2,1)}, bf16[512,256]{1,0:T(8,128)(2,1)S(1)}, u32[]{:S(2)}, u32[]{:S(2)}) collective-permute-start(bf16[512,256]{1,0:T(8,128)(2,1)} %param.5), channel_id=1, source_target_pairs={{0,1},{1,0},{2,3},{3,2},{4,5},{5,4},{6,7},{7,6},{8,9},{9,8},{10,11... | collective-permute-start | bytes 786440 | tf_op jit(solution)/shard_map/ppermute | solution.py:319
  3.6 18.0 %collective-permute-start.3 = (bf16[1024,256]{1,0:T(8,128)(2,1)S(1)}, bf16[1024,256]{1,0:T(8,128)(2,1)S(1)}, u32[]{:S(2)}, u32[]{:S(2)}) collective-permute-start(bf16[1024,256]{1,0:T(8,128)(2,1)S(1)} %constant_dynamic-slice_fusion.1.kv), channel_id=1, source_target_pairs={{1,5},{3,7},{4,0},{5,9},{6,2},{7,11},{8,4},{9,13},{10,6},{11,15},{... | collective-permute-start | bytes 1572872 | tf_op jit(solution)/shard_map/ppermute | solution.py:316
  4.9 17.1 %collective-permute-start.1 = (bf16[1024,256]{1,0:T(8,128)(2,1)S(1)}, bf16[1024,256]{1,0:T(8,128)(2,1)S(1)}, u32[]{:S(2)}, u32[]{:S(2)}) collective-permute-start(bf16[1024,256]{1,0:T(8,128)(2,1)S(1)} %constant_dynamic-slice_fusion.1.kv), channel_id=1, source_target_pairs={{0,2},{2,0},{3,5},{4,6},{5,3},{6,4},{7,9},{8,10},{9,7},{10,8},{11,... | collective-permute-start | bytes 1572872 | tf_op jit(solution)/shard_map/ppermute | solution.py:316
  9.8 15.1 %copy-start.2 = (bf16[512,1024]{1,0:T(8,128)(2,1)S(1)}, bf16[512,1024]{1,0:T(8,128)(2,1)}, u32[]{:S(2)}) copy-start(bf16[512,1024]{1,0:T(8,128)(2,1)} %g_ref.7) | copy-start | bytes 3145732
  9.8 12.4 %collective-permute-start.2 = (bf16[768,256]{1,0:T(8,128)(2,1)S(1)}, bf16[768,256]{1,0:T(8,128)(2,1)S(1)}, u32[]{:S(2)}, u32[]{:S(2)}) collective-permute-start(bf16[768,256]{1,0:T(8,128)(2,1)S(1)} %constant_dynamic-slice_fusion), channel_id=1, source_target_pairs={{0,6},{3,9},{4,10},{6,0},{7,13},{8,14},{9,3},{10,4},{13,7},{14,8},... | collective-permute-start | bytes 1179656 | tf_op jit(solution)/shard_map/ppermute | solution.py:316
  21.6 3.3 %collective-permute-start.6 = (bf16[1024,256]{1,0:T(8,128)(2,1)S(1)}, bf16[1024,256]{1,0:T(8,128)(2,1)S(1)}, u32[]{:S(2)}, u32[]{:S(2)}) collective-permute-start(bf16[1024,256]{1,0:T(8,128)(2,1)S(1)} %collective-permute-done.3.mine_2), channel_id=1, source_target_pairs={{0,1},{1,0},{2,3},{3,2},{4,5},{5,4},{6,7},{7,6},{8,9},{9,8},{10,11... | collective-permute-start | bytes 1572872 | tf_op jit(solution)/shard_map/ppermute | solution.py:319
  22.0 2.9 %collective-permute-start.4 = (bf16[1024,256]{1,0:T(8,128)(2,1)S(1)}, bf16[1024,256]{1,0:T(8,128)(2,1)S(1)}, u32[]{:S(2)}, u32[]{:S(2)}) collective-permute-start(bf16[1024,256]{1,0:T(8,128)(2,1)S(1)} %collective-permute-done.1.mine_0), channel_id=1, source_target_pairs={{0,1},{1,0},{2,3},{3,2},{4,5},{5,4},{6,7},{7,6},{8,9},{9,8},{10,11... | collective-permute-start | bytes 1572872 | tf_op jit(solution)/shard_map/ppermute | solution.py:319
  22.2 2.7 %collective-permute-start.5 = (bf16[768,256]{1,0:T(8,128)(2,1)S(1)}, bf16[768,256]{1,0:T(8,128)(2,1)S(1)}, u32[]{:S(2)}, u32[]{:S(2)}) collective-permute-start(bf16[768,256]{1,0:T(8,128)(2,1)S(1)} %collective-permute-done.2.mine_1), channel_id=1, source_target_pairs={{0,1},{1,0},{2,3},{3,2},{4,5},{5,4},{6,7},{7,6},{8,9},{9,8},{10,11... | collective-permute-start | bytes 1179656 | tf_op jit(solution)/shard_map/ppermute | solution.py:319
  29.3 0.6 copy-start.6
  30.0 23.0 %collective-permute-start.8 = (bf16[768,256]{1,0:T(8,128)(2,1)}, bf16[768,256]{1,0:T(8,128)(2,1)}, u32[]{:S(2)}, u32[]{:S(2)}) collective-permute-start(bf16[768,256]{1,0:T(8,128)(2,1)} %get-tuple-element.30), channel_id=1, source_target_pairs={{0,1},{1,0},{2,3},{3,2},{4,5},{5,4},{6,7},{7,6},{8,9},{9,8},{10,11... | collective-permute-start | bytes 1179656 | tf_op jit(solution)/shard_map/ppermute | solution.py:319
  51.3 3.2 %collective-permute-start.7 = (bf16[1024,256]{1,0:T(8,128)(2,1)}, bf16[1024,256]{1,0:T(8,128)(2,1)}, u32[]{:S(2)}, u32[]{:S(2)}) collective-permute-start(bf16[1024,256]{1,0:T(8,128)(2,1)} %get-tuple-element.28), channel_id=1, source_target_pairs={{0,1},{1,0},{2,3},{3,2},{4,5},{5,4},{6,7},{7,6},{8,9},{9,8},{10,11... | collective-permute-start | bytes 1572872 | tf_op jit(solution)/shard_map/ppermute | solution.py:319
  51.3 4.4 %collective-permute-start.9 = (bf16[1024,256]{1,0:T(8,128)(2,1)S(1)}, bf16[1024,256]{1,0:T(8,128)(2,1)}, u32[]{:S(2)}, u32[]{:S(2)}) collective-permute-start(bf16[1024,256]{1,0:T(8,128)(2,1)S(1)} %get-tuple-element.32), channel_id=1, source_target_pairs={{0,1},{1,0},{2,3},{3,2},{4,5},{5,4},{6,7},{7,6},{8,9},{9,8},{10,11... | collective-permute-start | bytes 1572872 | tf_op jit(solution)/shard_map/ppermute | solution.py:319
  52.9 33.5 %copy-start.3 = (bf16[512,1024]{1,0:T(8,128)(2,1)S(1)}, bf16[512,1024]{1,0:T(8,128)(2,1)}, u32[]{:S(2)}) copy-start(bf16[512,1024]{1,0:T(8,128)(2,1)} %g_ref.7) | copy-start | bytes 3145732
  52.9 33.5 %copy-start.5 = (f32[16,128,256]{2,1,0:T(8,128)S(1)}, f32[16,128,256]{2,1,0:T(8,128)}, u32[]{:S(2)}) copy-start(f32[16,128,256]{2,1,0:T(8,128)} %get-tuple-element.34.dq_in) | copy-start | bytes 6291460
  53.0 33.5 %copy-start.7 = (f32[16,8,256]{2,1,0:T(8,128)S(1)}, f32[16,8,256]{2,1,0:T(8,128)}, u32[]{:S(2)}) copy-start(f32[16,8,256]{2,1,0:T(8,128)} %copy-done.6) | copy-start | bytes 393220
  56.8 50.1 %collective-permute-start.11 = (bf16[768,256]{1,0:T(8,128)(2,1)S(1)}, bf16[768,256]{1,0:T(8,128)(2,1)S(1)}, u32[]{:S(2)}, u32[]{:S(2)}) collective-permute-start(bf16[768,256]{1,0:T(8,128)(2,1)S(1)} %add_convert_fusion.2), channel_id=1, source_target_pairs={{0,6},{3,9},{4,10},{6,0},{7,13},{8,14},{9,3},{10,4},{13,7},{14,8},... | collective-permute-start | bytes 1179656 | tf_op jit(solution)/shard_map/ppermute | solution.py:316
  84.5 22.4 %collective-permute-start.10 = (bf16[1024,256]{1,0:T(8,128)(2,1)S(1)}, bf16[1024,256]{1,0:T(8,128)(2,1)S(1)}, u32[]{:S(2)}, u32[]{:S(2)}) collective-permute-start(bf16[1024,256]{1,0:T(8,128)(2,1)S(1)} %add_convert_fusion.1), channel_id=1, source_target_pairs={{0,2},{2,0},{3,5},{4,6},{5,3},{6,4},{7,9},{8,10},{9,7},{10,8},{11,... | collective-permute-start | bytes 1572872 | tf_op jit(solution)/shard_map/ppermute | solution.py:316
  95.3 11.5 %collective-permute-start.12 = (bf16[1024,256]{1,0:T(8,128)(2,1)S(1)}, bf16[1024,256]{1,0:T(8,128)(2,1)S(1)}, u32[]{:S(2)}, u32[]{:S(2)}) collective-permute-start(bf16[1024,256]{1,0:T(8,128)(2,1)S(1)} %add_convert_fusion), channel_id=1, source_target_pairs={{0,4},{2,6},{4,8},{5,1},{6,10},{7,3},{8,12},{9,5},{10,14},{11,7},{... | collective-permute-start | bytes 1572872 | tf_op jit(solution)/shard_map/ppermute | solution.py:316
  107.3 1.6 %collective-permute-start.13 = (bf16[512,256]{1,0:T(8,128)(2,1)S(1)}, bf16[512,256]{1,0:T(8,128)(2,1)S(1)}, u32[]{:S(2)}, u32[]{:S(2)}) collective-permute-start(bf16[512,256]{1,0:T(8,128)(2,1)S(1)} %dynamic-slice_convert_fusion), channel_id=1, source_target_pairs={{0,1},{1,0},{2,3},{3,2},{4,5},{5,4},{6,7},{7,6},{8,9},{9,8},{10,11... | collective-permute-start | bytes 786440 | tf_op jit(solution)/shard_map/ppermute | solution.py:319

commit v3 on v2

--- a/solution.py
+++ b/solution.py
@@ -137,7 +137,7 @@
 
 def far_kernel(
     per_device, lengths, mine_0, mine_1, mine_2, twin_0, twin_1, twin_2, q_ref, g_ref, stats_in,
-    dq_out, stats_ref, mine_out_0, mine_out_1, mine_out_2, twin_out_0, twin_out_1, twin_out_2, kv, acc, low, exps, gprobs, maxes, keys_t, q_t, g_t, dq_ref, in_sems, out_sems, dq_sems,
+    dq_out, stats_out, mine_out_0, mine_out_1, mine_out_2, twin_out_0, twin_out_1, twin_out_2, kv, acc, low, exps, gprobs, maxes, keys_t, q_t, g_t, dq_ref, stats_ref, in_sems, out_sems, dq_sems, stats_sem,
 ):
     per_chip = 2 * per_device
     me = lax.axis_index("dp")
@@ -229,6 +229,8 @@
 
     lax.fori_loop(0, per_device * GROUPS, unit, 0)
 
+    stats_copy = pltpu.make_async_copy(stats_ref, stats_out, stats_sem)
+    stats_copy.start()
     low[...] = acc[...].astype(BF16)
     stores = []
     for number in range(len(ROUNDS)):
@@ -241,6 +243,7 @@
             stores[-1].start()
     for index in range(per_device * GROUPS):
         dq_copy(index).wait()
+    stats_copy.wait()
     for store in stores:
         store.wait()
 
@@ -352,9 +355,9 @@
     passed = tuple(jax.ShapeDtypeStruct(rows.shape, BF16) for rows in arrived)
     dq_far, stats, *partial = pl.pallas_call(
         functools.partial(far_kernel, per_device),
-        out_shape=(pltpu.HBM((slots, HD, TILE), F32), stats_shape) + passed + passed,
+        out_shape=(pltpu.HBM((slots, HD, TILE), F32), pltpu.HBM(stats_shape.shape, F32)) + passed + passed,
         in_specs=[smem] + [hbm] * 6 + [vmem, vmem, vmem],
-        out_specs=(pl.BlockSpec(memory_space=pltpu.HBM), vmem) + (hbm,) * 6,
+        out_specs=(pl.BlockSpec(memory_space=pltpu.HBM),) * 2 + (hbm,) * 6,
         scratch_shapes=[
             pltpu.VMEM((far_rows, 2 * HD), BF16),
             pltpu.VMEM((far_rows, 2 * HD), F32),
@@ -366,9 +369,11 @@
             turned,
             turned,
             pltpu.VMEM((slots, HD, TILE), F32),
+            pltpu.VMEM(stats_shape.shape, F32),
             pltpu.SemaphoreType.DMA((2, len(ROUNDS))),
             pltpu.SemaphoreType.DMA((2, len(ROUNDS))),
             pltpu.SemaphoreType.DMA((per_device * GROUPS,)),
+            pltpu.SemaphoreType.DMA,
         ],
         compiler_params=pltpu.CompilerParams(vmem_limit_bytes=43 * 2**20),
         cost_estimate=cost(40),
@@ -413,7 +418,7 @@
             name="own_grads",
         )(pair_lengths, chip, queries, grad_out, stats, dq_far, *before)
 
-    stats, *leaving = lax.optimization_barrier((stats, *leaving))
+    stats = lax.optimization_barrier((stats, *leaving[:-1]))[0]
     landed = [send(leaving[number], number, False) for number in range(len(ROUNDS) - 1)]
     grad_queries, own_grad = own_grads(0, stats, ())
     last, own_grad = lax.optimization_barrier((leaving[-1], own_grad))

time: 110 us -> 109 us (level)
  the two profiles are of different devices: /device:TPU:0 before, /device:TPU:31 now
where the time goes in v3:
time: 109 us; the launch traced here: 108 us
  starting transfers between devices  61.9 us (57%)
  Pallas kernels  32.1 us (29%)
  waiting for transfers between devices  5.46 us (5%)
  local copies, waits for them, and re-layouts  3.75 us (3%)
  other arithmetic  3.64 us (3%)
    ppermute x6, starting transfers between devices, send(): return lax.ppermute(value, 'dp', pairs)  53.8 us
    pallas_call x2, Pallas kernels, own_grads(): pl.pallas_call(functools.partial(own_grads_kernel, per_device, tile), out...  18 us
    pallas_call x1, Pallas kernels, body(): pl.pallas_call(functools.partial(own_stats_kernel, per_device), out_shape...  9.67 us
    ppermute x8, starting transfers between devices, to_twin(): return lax.ppermute(value, 'dp', [(i, i ^ 1) for i in range(count)])  8.12 us
    ppermute x8, waiting for transfers between devices, to_twin(): return lax.ppermute(value, 'dp', [(i, i ^ 1) for i in range(count)])  5.44 us
    pallas_call x1, Pallas kernels, body(): pl.pallas_call(functools.partial(far_kernel, per_device), out_shape=(pltp...  4.37 us
    unnamed x16, local copies, waits for them, and re-layouts  2.6 us
    convert_element_type x3, other arithmetic, body(): leaving.append(both.astype(BF16))  2.42 us
  transfers between devices with their start and end apart: 14, of which 4 were waited for; matrix products, arithmetic and copies ran while one was open for 3% of the time, Pallas kernels for 26%

profile of v3, /device:TPU:31, one launch (start us, length us, event | category | flops | bytes accessed | tf_op | source)
XLA Modules:
  0.0 107.6 jit_solution(13548296817186070480)
XLA Ops:
  0.6 0.0 copy-start.4
  0.6 0.0 copy-start.1
  0.7 0.0 copy-start
  0.7 0.7 collective-permute-start
  1.4 1.0 constant_dynamic-update-slice_fusion.2
  2.4 0.4 collective-permute-done
  2.8 1.0 constant_dynamic-update-slice_fusion
  3.8 1.3 %collective-permute-start.3 = (bf16[1024,256]{1,0:T(8,128)(2,1)S(1)}, bf16[1024,256]{1,0:T(8,128)(2,1)S(1)}, u32[]{:S(2)}, u32[]{:S(2)}) collective-permute-start(bf16[1024,256]{1,0:T(8,128)(2,1)S(1)} %constant_dynamic-slice_fusion.1.kv), channel_id=1, source_target_pairs={{1,5},{3,7},{4,0},{5,9},{6,2},{7,11},{8,4},{9,13},{10,6},{11,15},{... | collective-permute-start | bytes 1572872 | tf_op jit(solution)/shard_map/ppermute | solution.py:319
  5.1 0.7 collective-permute-start.1
  5.8 0.1 constant_dynamic-slice_fusion
  5.9 0.0 copy-start.2
  5.9 0.8 collective-permute-start.2
  6.8 0.0 copy-done.4
  6.8 0.0 copy-done.1
  6.8 0.0 copy-done
  6.8 9.7 %own_stats.1.stats_in = f32[16,8,256]{2,1,0:T(8,128)S(1)} custom-call(s32[10]{0:T(128)S(1)} %copy-done.4, bf16[1024,256]{1,0:T(8,128)(2,1)S(1)} %constant_dynamic-slice_fusion.1.kv, bf16[512,1024]{1,0:T(8,128)(2,1)S(1)} %copy-done, bf16[512,1024]{1,0:T(8,128)(2,1)S(1)} %copy-done.1), custom_call_target="tpu_custom_call" | custom-call | flops 6442450944 | bytes 8388608 | tf_op jit(solution)/shard_map/own_stats/pallas_call | solution.py:343
  16.5 0.0 collective-permute-done.3.mine_2
  16.5 5.9 %collective-permute-start.6 = (bf16[1024,256]{1,0:T(8,128)(2,1)S(1)}, bf16[1024,256]{1,0:T(8,128)(2,1)S(1)}, u32[]{:S(2)}, u32[]{:S(2)}) collective-permute-start(bf16[1024,256]{1,0:T(8,128)(2,1)S(1)} %collective-permute-done.3.mine_2), channel_id=1, source_target_pairs={{0,1},{1,0},{2,3},{3,2},{4,5},{5,4},{6,7},{7,6},{8,9},{9,8},{10,11... | collective-permute-start | bytes 1572872 | tf_op jit(solution)/shard_map/ppermute | solution.py:322
  22.3 0.0 collective-permute-done.1.mine_0
  22.3 0.1 collective-permute-start.4
  22.4 0.0 collective-permute-done.2.mine_1
  22.4 0.4 collective-permute-start.5
  22.9 2.3 %collective-permute-done.5.twin_1 = bf16[768,256]{1,0:T(8,128)(2,1)S(1)} collective-permute-done((bf16[768,256]{1,0:T(8,128)(2,1)S(1)}, bf16[768,256]{1,0:T(8,128)(2,1)S(1)}, u32[]{:S(2)}, u32[]{:S(2)}) %collective-permute-start.5) | collective-permute-done | bytes 393248 | tf_op jit(solution)/shard_map/ppermute | solution.py:322
  25.2 0.0 collective-permute-done.6.twin_2
  25.2 0.0 collective-permute-done.4.twin_0
  25.2 4.4 %far.1 = (f32[16,128,256]{2,1,0:T(8,128)}, f32[16,8,256]{2,1,0:T(8,128)}, bf16[1024,256]{1,0:T(8,128)(2,1)S(1)}, bf16[768,256]{1,0:T(8,128)(2,1)S(1)}, bf16[1024...) custom-call(s32[10]{0:T(128)S(1)} %copy-done.4, ...), custom_call_target="tpu_custom_call" | custom-call | flops 32212254720 | bytes 8388608 | tf_op jit(solution)/shard_map/far/pallas_call | solution.py:356
  29.6 0.4 collective-permute-start.8
  30.0 0.1 collective-permute-start.7
  30.2 0.4 collective-permute-start.9
  30.5 1.2 %collective-permute-done.8 = bf16[768,256]{1,0:T(8,128)(2,1)} collective-permute-done((bf16[768,256]{1,0:T(8,128)(2,1)}, bf16[768,256]{1,0:T(8,128)(2,1)}, u32[]{:S(2)}, u32[]{:S(2)}) %collective-permute-start.8) | collective-permute-done | bytes 393248 | tf_op jit(solution)/shard_map/ppermute | solution.py:322
  31.7 1.1 %add_convert_fusion.2 = bf16[768,256]{1,0:T(8,128)(2,1)S(1)} fusion(bf16[768,256]{1,0:T(8,128)(2,1)} %collective-permute-done.8, bf16[768,256]{1,0:T(8,128)(2,1)S(1)} %get-tuple-element.26), kind=kLoop, calls=%fused_computation.3 | loop fusion | flops 786432 | bytes 1179648 | tf_op jit(solution)/shard_map/convert_element_type | solution.py:386
  32.8 0.7 collective-permute-start.11
  33.5 0.0 collective-permute-done.7
  33.5 1.2 %add_convert_fusion.1 = bf16[1024,256]{1,0:T(8,128)(2,1)S(1)} fusion(bf16[1024,256]{1,0:T(8,128)(2,1)} %collective-permute-done.7, bf16[1024,256]{1,0:T(8,128)(2,1)S(1)} %get-tuple-element.24), kind=kLoop, calls=%fused_computation.2 | loop fusion | flops 1048576 | bytes 1572864 | tf_op jit(solution)/shard_map/convert_element_type | solution.py:386
  34.7 0.7 collective-permute-start.10
  35.4 1.6 %copy-done.5 = f32[16,128,256]{2,1,0:T(8,128)S(1)} copy-done((f32[16,128,256]{2,1,0:T(8,128)S(1)}, f32[16,128,256]{2,1,0:T(8,128)}, u32[]{:S(2)}) %copy-start.5) | copy-done | bytes 2097176
  37.0 9.0 %own_grads.2 = (bf16[512,1024]{1,0:T(8,128)(2,1)}, f32[1024,256]{1,0:T(8,128)S(1)}) custom-call(s32[10]{0:T(128)S(1)} %copy-done.4, bf16[1024,256]{1,0:T(8,128)(2,1)S(1)} %constant_dynamic-slice_fusion.1.kv, bf16[512,1024]{1,0:T(8,128)(2,1)S(1)} %copy-done, bf16[512,1024]{1,0:T(8,128)(2,1)S(1)} %copy-done.3, f32[16,8,256]{2,1,0:T(8,128)S(1)} %copy-done.6, ...), custom_call_target="tpu_custom_call" | custom-call | flops 8053063680 | bytes 8388608 | tf_op jit(solution)/shard_map/own_grads/pallas_call | solution.py:392
  46.0 0.0 collective-permute-done.9
  46.0 0.2 add_convert_fusion
  46.1 49.6 %collective-permute-start.12 = (bf16[1024,256]{1,0:T(8,128)(2,1)S(1)}, bf16[1024,256]{1,0:T(8,128)(2,1)S(1)}, u32[]{:S(2)}, u32[]{:S(2)}) collective-permute-start(bf16[1024,256]{1,0:T(8,128)(2,1)S(1)} %add_convert_fusion), channel_id=1, source_target_pairs={{0,4},{2,6},{4,8},{5,1},{6,10},{7,3},{8,12},{9,5},{10,14},{11,7},{... | collective-permute-start | bytes 1572872 | tf_op jit(solution)/shard_map/ppermute | solution.py:319
  95.7 9.0 %own_grads.3 = (bf16[512,1024]{1,0:T(8,128)(2,1)}, f32[1024,256]{1,0:T(8,128)S(1)}) custom-call(s32[10]{0:T(128)S(1)} %copy-done.4, bf16[1024,256]{1,0:T(8,128)(2,1)S(1)} %constant_dynamic-slice_fusion.1.kv, bf16[512,1024]{1,0:T(8,128)(2,1)S(1)} %copy-done, bf16[512,1024]{1,0:T(8,128)(2,1)S(1)} %copy-done.3, ...), custom_call_target="tpu_custom_call", output_to_operand_aliasing={{0}: (7, {})} | custom-call | flops 8053063680 | bytes 8388608 | tf_op jit(solution)/shard_map/own_grads/pallas_call | solution.py:392
  104.8 0.0 collective-permute-done.11
  104.8 0.0 collective-permute-done.10
  104.8 0.0 collective-permute-done.12
  104.8 0.4 convert_add_fusion
  105.2 0.1 collective-permute-start.13
  105.3 1.5 %collective-permute-done.13 = bf16[512,256]{1,0:T(8,128)(2,1)S(1)} collective-permute-done((bf16[512,256]{1,0:T(8,128)(2,1)S(1)}, bf16[512,256]{1,0:T(8,128)(2,1)S(1)}, u32[]{:S(2)}, u32[]{:S(2)}) %collective-permute-start.13) | collective-permute-done | bytes 262176 | tf_op jit(solution)/shard_map/ppermute | solution.py:322
  106.8 0.8 convert_add_fusion.1
  (9 shorter events, 0.1 us)
Async XLA Ops:
  0.6 6.1 %copy-start.4 = (s32[10]{0:T(128)S(1)}, s32[10]{0:T(128)}, u32[]{:S(2)}) copy-start(s32[10]{0:T(128)} %lengths.7) | copy-start | bytes 124
  0.6 6.1 %copy-start.1 = (bf16[512,1024]{1,0:T(8,128)(2,1)S(1)}, bf16[512,1024]{1,0:T(8,128)(2,1)}, u32[]{:S(2)}) copy-start(bf16[512,1024]{1,0:T(8,128)(2,1)} %g_ref.7) | copy-start | bytes 3145732
  0.7 6.1 %copy-start = (bf16[512,1024]{1,0:T(8,128)(2,1)S(1)}, bf16[512,1024]{1,0:T(8,128)(2,1)}, u32[]{:S(2)}) copy-start(bf16[512,1024]{1,0:T(8,128)(2,1)} %q_ref.7) | copy-start | bytes 3145732
  0.7 2.1 %collective-permute-start = (bf16[512,256]{1,0:T(8,128)(2,1)}, bf16[512,256]{1,0:T(8,128)(2,1)S(1)}, u32[]{:S(2)}, u32[]{:S(2)}) collective-permute-start(bf16[512,256]{1,0:T(8,128)(2,1)} %param.5), channel_id=1, source_target_pairs={{0,1},{1,0},{2,3},{3,2},{4,5},{5,4},{6,7},{7,6},{8,9},{9,8},{10,11... | collective-permute-start | bytes 786440 | tf_op jit(solution)/shard_map/ppermute | solution.py:322
  3.8 12.7 %collective-permute-start.3 = (bf16[1024,256]{1,0:T(8,128)(2,1)S(1)}, bf16[1024,256]{1,0:T(8,128)(2,1)S(1)}, u32[]{:S(2)}, u32[]{:S(2)}) collective-permute-start(bf16[1024,256]{1,0:T(8,128)(2,1)S(1)} %constant_dynamic-slice_fusion.1.kv), channel_id=1, source_target_pairs={{1,5},{3,7},{4,0},{5,9},{6,2},{7,11},{8,4},{9,13},{10,6},{11,15},{... | collective-permute-start | bytes 1572872 | tf_op jit(solution)/shard_map/ppermute | solution.py:319
  5.1 17.2 %collective-permute-start.1 = (bf16[1024,256]{1,0:T(8,128)(2,1)S(1)}, bf16[1024,256]{1,0:T(8,128)(2,1)S(1)}, u32[]{:S(2)}, u32[]{:S(2)}) collective-permute-start(bf16[1024,256]{1,0:T(8,128)(2,1)S(1)} %constant_dynamic-slice_fusion.1.kv), channel_id=1, source_target_pairs={{0,2},{2,0},{3,5},{4,6},{5,3},{6,4},{7,9},{8,10},{9,7},{10,8},{11,... | collective-permute-start | bytes 1572872 | tf_op jit(solution)/shard_map/ppermute | solution.py:319
  5.9 19.3 %copy-start.2 = (bf16[512,1024]{1,0:T(8,128)(2,1)S(1)}, bf16[512,1024]{1,0:T(8,128)(2,1)}, u32[]{:S(2)}) copy-start(bf16[512,1024]{1,0:T(8,128)(2,1)} %g_ref.7) | copy-start | bytes 3145732
  5.9 16.5 %collective-permute-start.2 = (bf16[768,256]{1,0:T(8,128)(2,1)S(1)}, bf16[768,256]{1,0:T(8,128)(2,1)S(1)}, u32[]{:S(2)}, u32[]{:S(2)}) collective-permute-start(bf16[768,256]{1,0:T(8,128)(2,1)S(1)} %constant_dynamic-slice_fusion), channel_id=1, source_target_pairs={{0,6},{3,9},{4,10},{6,0},{7,13},{8,14},{9,3},{10,4},{13,7},{14,8},... | collective-permute-start | bytes 1179656 | tf_op jit(solution)/shard_map/ppermute | solution.py:319
  16.5 8.7 %collective-permute-start.6 = (bf16[1024,256]{1,0:T(8,128)(2,1)S(1)}, bf16[1024,256]{1,0:T(8,128)(2,1)S(1)}, u32[]{:S(2)}, u32[]{:S(2)}) collective-permute-start(bf16[1024,256]{1,0:T(8,128)(2,1)S(1)} %collective-permute-done.3.mine_2), channel_id=1, source_target_pairs={{0,1},{1,0},{2,3},{3,2},{4,5},{5,4},{6,7},{7,6},{8,9},{9,8},{10,11... | collective-permute-start | bytes 1572872 | tf_op jit(solution)/shard_map/ppermute | solution.py:322
  22.3 2.9 %collective-permute-start.4 = (bf16[1024,256]{1,0:T(8,128)(2,1)S(1)}, bf16[1024,256]{1,0:T(8,128)(2,1)S(1)}, u32[]{:S(2)}, u32[]{:S(2)}) collective-permute-start(bf16[1024,256]{1,0:T(8,128)(2,1)S(1)} %collective-permute-done.1.mine_0), channel_id=1, source_target_pairs={{0,1},{1,0},{2,3},{3,2},{4,5},{5,4},{6,7},{7,6},{8,9},{9,8},{10,11... | collective-permute-start | bytes 1572872 | tf_op jit(solution)/shard_map/ppermute | solution.py:322
  22.4 2.8 %collective-permute-start.5 = (bf16[768,256]{1,0:T(8,128)(2,1)S(1)}, bf16[768,256]{1,0:T(8,128)(2,1)S(1)}, u32[]{:S(2)}, u32[]{:S(2)}) collective-permute-start(bf16[768,256]{1,0:T(8,128)(2,1)S(1)} %collective-permute-done.2.mine_1), channel_id=1, source_target_pairs={{0,1},{1,0},{2,3},{3,2},{4,5},{5,4},{6,7},{7,6},{8,9},{9,8},{10,11... | collective-permute-start | bytes 1179656 | tf_op jit(solution)/shard_map/ppermute | solution.py:322
  29.6 2.1 %collective-permute-start.8 = (bf16[768,256]{1,0:T(8,128)(2,1)}, bf16[768,256]{1,0:T(8,128)(2,1)}, u32[]{:S(2)}, u32[]{:S(2)}) collective-permute-start(bf16[768,256]{1,0:T(8,128)(2,1)} %get-tuple-element.27), channel_id=1, source_target_pairs={{0,1},{1,0},{2,3},{3,2},{4,5},{5,4},{6,7},{7,6},{8,9},{9,8},{10,11... | collective-permute-start | bytes 1179656 | tf_op jit(solution)/shard_map/ppermute | solution.py:322
  30.0 3.5 %collective-permute-start.7 = (bf16[1024,256]{1,0:T(8,128)(2,1)}, bf16[1024,256]{1,0:T(8,128)(2,1)}, u32[]{:S(2)}, u32[]{:S(2)}) collective-permute-start(bf16[1024,256]{1,0:T(8,128)(2,1)} %get-tuple-element.25), channel_id=1, source_target_pairs={{0,1},{1,0},{2,3},{3,2},{4,5},{5,4},{6,7},{7,6},{8,9},{9,8},{10,11... | collective-permute-start | bytes 1572872 | tf_op jit(solution)/shard_map/ppermute | solution.py:322
  30.2 5.2 %copy-start.3 = (bf16[512,1024]{1,0:T(8,128)(2,1)S(1)}, bf16[512,1024]{1,0:T(8,128)(2,1)}, u32[]{:S(2)}) copy-start(bf16[512,1024]{1,0:T(8,128)(2,1)} %g_ref.7) | copy-start | bytes 3145732
  30.2 5.2 %copy-start.6 = (f32[16,8,256]{2,1,0:T(8,128)S(1)}, f32[16,8,256]{2,1,0:T(8,128)}, u32[]{:S(2)}) copy-start(f32[16,8,256]{2,1,0:T(8,128)} %get-tuple-element.28.stats_ref) | copy-start | bytes 393220
  30.2 15.8 %collective-permute-start.9 = (bf16[1024,256]{1,0:T(8,128)(2,1)S(1)}, bf16[1024,256]{1,0:T(8,128)(2,1)S(1)}, u32[]{:S(2)}, u32[]{:S(2)}) collective-permute-start(bf16[1024,256]{1,0:T(8,128)(2,1)S(1)} %get-tuple-element.31), channel_id=1, source_target_pairs={{0,1},{1,0},{2,3},{3,2},{4,5},{5,4},{6,7},{7,6},{8,9},{9,8},{10,11... | collective-permute-start | bytes 1572872 | tf_op jit(solution)/shard_map/ppermute | solution.py:322
  32.8 72.0 %collective-permute-start.11 = (bf16[768,256]{1,0:T(8,128)(2,1)S(1)}, bf16[768,256]{1,0:T(8,128)(2,1)S(1)}, u32[]{:S(2)}, u32[]{:S(2)}) collective-permute-start(bf16[768,256]{1,0:T(8,128)(2,1)S(1)} %add_convert_fusion.2), channel_id=1, source_target_pairs={{0,6},{3,9},{4,10},{6,0},{7,13},{8,14},{9,3},{10,4},{13,7},{14,8},... | collective-permute-start | bytes 1179656 | tf_op jit(solution)/shard_map/ppermute | solution.py:319
  34.7 70.1 %collective-permute-start.10 = (bf16[1024,256]{1,0:T(8,128)(2,1)S(1)}, bf16[1024,256]{1,0:T(8,128)(2,1)S(1)}, u32[]{:S(2)}, u32[]{:S(2)}) collective-permute-start(bf16[1024,256]{1,0:T(8,128)(2,1)S(1)} %add_convert_fusion.1), channel_id=1, source_target_pairs={{0,2},{2,0},{3,5},{4,6},{5,3},{6,4},{7,9},{8,10},{9,7},{10,8},{11,... | collective-permute-start | bytes 1572872 | tf_op jit(solution)/shard_map/ppermute | solution.py:319
  35.4 1.6 %copy-start.5 = (f32[16,128,256]{2,1,0:T(8,128)S(1)}, f32[16,128,256]{2,1,0:T(8,128)}, u32[]{:S(2)}) copy-start(f32[16,128,256]{2,1,0:T(8,128)} %get-tuple-element.29.dq_in) | copy-start | bytes 6291460
  46.1 58.6 %collective-permute-start.12 = (bf16[1024,256]{1,0:T(8,128)(2,1)S(1)}, bf16[1024,256]{1,0:T(8,128)(2,1)S(1)}, u32[]{:S(2)}, u32[]{:S(2)}) collective-permute-start(bf16[1024,256]{1,0:T(8,128)(2,1)S(1)} %add_convert_fusion), channel_id=1, source_target_pairs={{0,4},{2,6},{4,8},{5,1},{6,10},{7,3},{8,12},{9,5},{10,14},{11,7},{... | collective-permute-start | bytes 1572872 | tf_op jit(solution)/shard_map/ppermute | solution.py:319
  105.2 1.6 %collective-permute-start.13 = (bf16[512,256]{1,0:T(8,128)(2,1)S(1)}, bf16[512,256]{1,0:T(8,128)(2,1)S(1)}, u32[]{:S(2)}, u32[]{:S(2)}) collective-permute-start(bf16[512,256]{1,0:T(8,128)(2,1)S(1)} %dynamic-slice_convert_fusion), channel_id=1, source_target_pairs={{0,1},{1,0},{2,3},{3,2},{4,5},{5,4},{6,7},{7,6},{8,9},{9,8},{10,11... | collective-permute-start | bytes 786440 | tf_op jit(solution)/shard_map/ppermute | solution.py:322
